TPU v7x, 32 devices: a whole 2x2x4 slice. The times are simulated.
32 devices in a mesh: seq: 16 (over z, x, core), wsh: 2 (over y).
Axes of the slice: x: 2, y: 2, z: 4, core: 2. Of those that a mesh axis runs over, the one named last changes fastest.
Arguments:
- tokens: bfloat16 [8, 2048, 640], P('wsh', 'seq'), may hold values from -6 to 6
- group_offset: int32 [8, 16], P('wsh', 'seq'), may hold values from 0 to 1920, as said below
- q_weight: bfloat16 [2, 1024, 640], P(None, ('seq', 'wsh')), may hold values from -0.25 to 0.25
- k_weight: bfloat16 [2, 256, 640], P(None, ('seq', 'wsh')), may hold values from -0.25 to 0.25
- v_weight: bfloat16 [2, 256, 640], P(None, ('seq', 'wsh')), may hold values from -0.25 to 0.25
- o_weight: bfloat16 [2, 1024, 640], P(None, ('seq', 'wsh')), may hold values from -0.1875 to 0.1875
- gate_weight: bfloat16 [2, 2048, 640], P(None, ('seq', 'wsh')), may hold values from -0.25 to 0.25
- up_weight: bfloat16 [2, 2048, 640], P(None, ('seq', 'wsh')), may hold values from -0.25 to 0.25
- down_weight: bfloat16 [2, 2048, 640], P(None, ('seq', 'wsh')), may hold values from -0.125 to 0.125
- norm_gains: float32 [2, 4, 640], replicated, may hold values from 0.1 to 1.9
- head_gains: float32 [2, 2, 256], replicated, may hold values from 0.1 to 1.9
- out_grad: bfloat16 [8, 2048, 640], P('wsh', 'seq'), may hold values from -6 to 6
Outputs:
- block_out: bfloat16 [8, 2048, 640], P('wsh', 'seq')
- input_grad: float32 [8, 2048, 640], P('wsh', 'seq')
- q_grad: float32 [2, 1024, 640], P(None, ('seq', 'wsh'))
- k_grad: float32 [2, 256, 640], P(None, ('seq', 'wsh'))
- v_grad: float32 [2, 256, 640], P(None, ('seq', 'wsh'))
- o_grad: float32 [2, 1024, 640], P(None, ('seq', 'wsh'))
- gate_grad: float32 [2, 2048, 640], P(None, ('seq', 'wsh'))
- up_grad: float32 [2, 2048, 640], P(None, ('seq', 'wsh'))
- down_grad: float32 [2, 2048, 640], P(None, ('seq', 'wsh'))
- norm_grad: float32 [2, 4, 640], replicated
- head_grad: float32 [2, 2, 256], replicated
Inputs may be any that keep to these rules, and one draw needn't show every extreme that they name: `group_offset`: each row is one sequence or two laid end to end; every sequence starts at a multiple of 128, so a value is 128 times the group's index within its sequence; the first group of each row has 0. Among the 4 rows of each index of wsh, one is a single sequence.
All inputs are finite; a program needn't handle non-finite values.
Results may differ from a plain program's by a relative error of at most 0.028.
Values may be sent and summed in bfloat16 or wider, within the bound.
A program may use at most 192 MiB of HBM per device.

v0:
```python
import jax
import jax.numpy as jnp
from jax import lax
from jax.sharding import PartitionSpec as P

WINDOW = 512


EPSILON = 1e-06
ROPE_BASE = 10000.0
MASKED = -1e30


def shifted(value, axis, steps):
    count = lax.axis_size(axis)
    initial, last = (max(0, -steps), min(count, count - steps))
    return lax.ppermute(value, axis, [(source, source + steps) for source in range(initial, last)])


def norm_gain(values, scaling):
    return values * lax.rsqrt(jnp.mean(values * values, axis=-1, keepdims=True) + EPSILON) * scaling


def rotate(values, angles):
    half_width = values.shape[-1] // 2
    leading = values[..., :half_width]
    trailing = values[..., half_width:]
    cosine = jnp.cos(angles)
    sine_part = jnp.sin(angles)
    return jnp.concatenate(
        [leading * cosine - trailing * sine_part, trailing * cosine + leading * sine_part], axis=-1
    )


def frequencies(head_width):
    indices = jnp.arange(head_width // 2).astype(jnp.float32)
    return ROPE_BASE ** (-2.0 * indices / head_width)


def gelu_product(gate_in, up_in):
    return jax.nn.gelu(gate_in, approximate=True) * up_in


def query_rot(q_lin, head_gain, angles, head_count):
    shaped = q_lin.reshape(q_lin.shape[0], q_lin.shape[1], head_count, -1)
    return rotate(norm_gain(shaped, head_gain), angles[:, :, None, :]) * shaped.shape[-1] ** (-0.5)


def key_rot(k_lin, head_gain, angles):
    return rotate(norm_gain(k_lin, head_gain), angles)


def layer_weights(weights, layer_idx):
    q_rows, k_rows, v_rows, o_rows, gate_rows, up_rows, down_rows = weights
    return (
        lax.all_gather(q_rows[layer_idx], ("seq", "wsh"), axis=0, tiled=True),
        lax.all_gather(k_rows[layer_idx], ("seq", "wsh"), axis=0, tiled=True),
        lax.all_gather(v_rows[layer_idx], ("seq", "wsh"), axis=0, tiled=True),
        lax.all_gather(o_rows[layer_idx], ("seq", "wsh"), axis=0, tiled=True),
        lax.all_gather(gate_rows[layer_idx], ("seq", "wsh"), axis=0, tiled=True),
        lax.all_gather(up_rows[layer_idx], ("seq", "wsh"), axis=0, tiled=True),
        lax.all_gather(down_rows[layer_idx], ("seq", "wsh"), axis=0, tiled=True),
    )


def share_grads(grads):
    seq_count = lax.axis_size("seq")
    wsh_count = lax.axis_size("wsh")
    shaped = [
        member.reshape(
            seq_count, wsh_count, member.shape[0] // (seq_count * wsh_count), member.shape[1]
        )
        for member in grads
    ]
    dw_query, dw_key, dw_value, dw_output, dw_gate, dw_up, dw_down = shaped
    moved = (
        lax.all_to_all(
            dw_query.astype(jnp.bfloat16), "seq", split_axis=0, concat_axis=0, tiled=True
        ).astype(dw_query.dtype),
        lax.all_to_all(
            dw_key.astype(jnp.bfloat16), "seq", split_axis=0, concat_axis=0, tiled=True
        ).astype(dw_key.dtype),
        lax.all_to_all(
            dw_value.astype(jnp.bfloat16), "seq", split_axis=0, concat_axis=0, tiled=True
        ).astype(dw_value.dtype),
        lax.all_to_all(
            dw_output.astype(jnp.bfloat16), "seq", split_axis=0, concat_axis=0, tiled=True
        ).astype(dw_output.dtype),
        lax.all_to_all(
            dw_gate.astype(jnp.bfloat16), "seq", split_axis=0, concat_axis=0, tiled=True
        ).astype(dw_gate.dtype),
        lax.all_to_all(
            dw_up.astype(jnp.bfloat16), "seq", split_axis=0, concat_axis=0, tiled=True
        ).astype(dw_up.dtype),
        lax.all_to_all(
            dw_down.astype(jnp.bfloat16), "seq", split_axis=0, concat_axis=0, tiled=True
        ).astype(dw_down.dtype),
    )
    dw_query, dw_key, dw_value, dw_output, dw_gate, dw_up, dw_down = [
        jnp.sum(member, axis=0) for member in moved
    ]
    moved = (
        lax.all_to_all(
            dw_query.astype(jnp.bfloat16), "wsh", split_axis=0, concat_axis=0, tiled=True
        ).astype(dw_query.dtype),
        lax.all_to_all(
            dw_key.astype(jnp.bfloat16), "wsh", split_axis=0, concat_axis=0, tiled=True
        ).astype(dw_key.dtype),
        lax.all_to_all(
            dw_value.astype(jnp.bfloat16), "wsh", split_axis=0, concat_axis=0, tiled=True
        ).astype(dw_value.dtype),
        lax.all_to_all(
            dw_output.astype(jnp.bfloat16), "wsh", split_axis=0, concat_axis=0, tiled=True
        ).astype(dw_output.dtype),
        lax.all_to_all(
            dw_gate.astype(jnp.bfloat16), "wsh", split_axis=0, concat_axis=0, tiled=True
        ).astype(dw_gate.dtype),
        lax.all_to_all(
            dw_up.astype(jnp.bfloat16), "wsh", split_axis=0, concat_axis=0, tiled=True
        ).astype(dw_up.dtype),
        lax.all_to_all(
            dw_down.astype(jnp.bfloat16), "wsh", split_axis=0, concat_axis=0, tiled=True
        ).astype(dw_down.dtype),
    )
    return tuple((jnp.sum(member, axis=0) for member in moved))


def earlier_keys(packed_tokens, hop_count):
    pieces = []
    moving = packed_tokens
    for hop_idx in range(hop_count):
        moving = shifted(moving, "seq", 1)
        pieces.insert(0, moving)
    return jnp.concatenate(pieces + [packed_tokens], axis=1)


def returned_grads(grad_all, hop_count, group_len):
    slices = [
        grad_all[:, (hop_count - hop_idx) * group_len : (hop_count - hop_idx + 1) * group_len]
        for hop_idx in range(hop_count + 1)
    ]
    summed = slices[0]
    moving = slices[hop_count]
    for hop_idx in range(hop_count, 0, -1):
        moving = shifted(moving.astype(jnp.bfloat16), "seq", -1).astype(moving.dtype)
        if hop_idx > 1:
            moving = moving + slices[hop_idx - 1]
    summed = summed + moving
    return summed


def masked_scores(rotated_query, key_matrix_rows, allowed):
    attention_scores = jnp.einsum(
        "uzmt,upt->umzp", rotated_query, key_matrix_rows, preferred_element_type=jnp.float32
    )
    return jnp.where(allowed[:, None], attention_scores, MASKED)


def forward_layer(stream, gathered, gains, head_gain, angles, allowed, hop_count):
    q_mat, k_mat, v_mat, o_mat, gate_mat, up_mat, down_mat = gathered
    head_width = head_gain.shape[-1]
    head_count = q_mat.shape[0] // head_width
    batch_rows, group_len = (stream.shape[0], stream.shape[1])
    normed = norm_gain(stream, gains[0]).astype(jnp.bfloat16)
    q_lin = jnp.einsum("bcd,ed->bce", normed, q_mat, preferred_element_type=jnp.float32)
    k_lin = jnp.einsum("bcd,ed->bce", normed, k_mat, preferred_element_type=jnp.float32)
    v_val = jnp.einsum("bcd,ed->bce", normed, v_mat, preferred_element_type=jnp.float32).astype(
        jnp.bfloat16
    )
    rotated_query = query_rot(q_lin, head_gain[0], angles, head_count).astype(jnp.bfloat16)
    k_rot = key_rot(k_lin, head_gain[1], angles).astype(jnp.bfloat16)
    packed_tokens = earlier_keys(jnp.concatenate([k_rot, v_val], axis=-1), hop_count)
    attention_scores = masked_scores(rotated_query, packed_tokens[..., :head_width], allowed)
    row_max = jnp.max(attention_scores, axis=-1, keepdims=True)
    log_total = row_max + jnp.log(
        jnp.sum(jnp.exp(attention_scores - row_max), axis=-1, keepdims=True)
    )
    probabilities_bfloat = jnp.exp(attention_scores - log_total).astype(jnp.bfloat16)
    mixed = jnp.einsum(
        "faln,fnv->flav",
        probabilities_bfloat,
        packed_tokens[..., head_width:],
        preferred_element_type=jnp.float32,
    )
    mixed = mixed.reshape(batch_rows, group_len, head_count * head_width).astype(jnp.bfloat16)
    attn_out = jnp.einsum("bce,ed->bcd", mixed, o_mat, preferred_element_type=jnp.float32)
    after_attn = stream + norm_gain(attn_out, gains[1])
    hidden = norm_gain(after_attn, gains[2]).astype(jnp.bfloat16)
    gate_pre = jnp.einsum("bcd,fd->bcf", hidden, gate_mat, preferred_element_type=jnp.float32)
    up_pre = jnp.einsum("bcd,fd->bcf", hidden, up_mat, preferred_element_type=jnp.float32)
    activated = gelu_product(gate_pre, up_pre).astype(jnp.bfloat16)
    down_out = jnp.einsum("bcf,fd->bcd", activated, down_mat, preferred_element_type=jnp.float32)
    layer_out = after_attn + norm_gain(down_out, gains[3])
    saved = (
        stream,
        normed,
        q_lin,
        k_lin,
        rotated_query,
        packed_tokens,
        log_total,
        mixed,
        attn_out,
        after_attn,
        hidden,
        gate_pre,
        up_pre,
        activated,
        down_out,
    )
    return (saved, layer_out)


def backward_layer(upstream, saved, gathered, gains, head_gain, angles, allowed, hop_count):
    (
        stream,
        normed,
        q_lin,
        k_lin,
        rotated_query,
        packed_tokens,
        log_total,
        mixed,
        attn_out,
        after_attn,
        hidden,
        gate_pre,
        up_pre,
        activated,
        down_out,
    ) = saved
    q_mat, k_mat, v_mat, o_mat, gate_mat, up_mat, down_mat = gathered
    head_width = head_gain.shape[-1]
    head_count = q_mat.shape[0] // head_width
    batch_rows, group_len = (stream.shape[0], stream.shape[1])
    unused, pullback = jax.vjp(norm_gain, down_out, gains[3])
    d_down, g_post_ff = pullback(upstream)
    d_down = d_down.astype(jnp.bfloat16)
    dw_down = jnp.einsum("bcf,bcd->fd", activated, d_down, preferred_element_type=jnp.float32)
    d_act = jnp.einsum("bcd,fd->bcf", d_down, down_mat, preferred_element_type=jnp.float32)
    unused, pullback = jax.vjp(gelu_product, gate_pre, up_pre)
    d_gate, d_up = pullback(d_act)
    d_gate = d_gate.astype(jnp.bfloat16)
    d_up = d_up.astype(jnp.bfloat16)
    dw_gate = jnp.einsum("bcf,bcd->fd", d_gate, hidden, preferred_element_type=jnp.float32)
    dw_up = jnp.einsum("bcf,bcd->fd", d_up, hidden, preferred_element_type=jnp.float32)
    d_hidden = jnp.einsum(
        "bcf,fd->bcd", d_gate, gate_mat, preferred_element_type=jnp.float32
    ) + jnp.einsum("bcf,fd->bcd", d_up, up_mat, preferred_element_type=jnp.float32)
    unused, pullback = jax.vjp(norm_gain, after_attn, gains[2])
    d_after, g_pre_ff = pullback(d_hidden)
    d_after = upstream + d_after
    unused, pullback = jax.vjp(norm_gain, attn_out, gains[1])
    d_attn, g_post_attn = pullback(d_after)
    d_attn = d_attn.astype(jnp.bfloat16)
    dw_output = jnp.einsum("bce,bcd->ed", mixed, d_attn, preferred_element_type=jnp.float32)
    mixed_gradient = jnp.einsum(
        "bcd,ed->bce", d_attn, o_mat, preferred_element_type=jnp.float32
    ).astype(jnp.bfloat16)
    mixed_gradient = mixed_gradient.reshape(batch_rows, group_len, head_count, head_width)
    key_matrix_rows = packed_tokens[..., :head_width]
    value_matrix_rows = packed_tokens[..., head_width:]
    attention_probabilities = jnp.exp(
        masked_scores(rotated_query, key_matrix_rows, allowed) - log_total
    )
    probability_gradient = jnp.einsum(
        "uzmt,upt->umzp", mixed_gradient, value_matrix_rows, preferred_element_type=jnp.float32
    )
    score_gradient = (
        attention_probabilities
        * (
            probability_gradient
            - jnp.sum(probability_gradient * attention_probabilities, axis=-1, keepdims=True)
        )
    ).astype(jnp.bfloat16)
    rotated_query_gradient = jnp.einsum(
        "faln,fnv->flav", score_gradient, key_matrix_rows, preferred_element_type=jnp.float32
    )
    key_gradient_rows = jnp.einsum(
        "tznj,tnzq->tjq", score_gradient, rotated_query, preferred_element_type=jnp.float32
    )
    d_values = jnp.einsum(
        "tznj,tnzq->tjq",
        attention_probabilities.astype(jnp.bfloat16),
        mixed_gradient,
        preferred_element_type=jnp.float32,
    )
    d_packed = returned_grads(
        jnp.concatenate([key_gradient_rows, d_values], axis=-1), hop_count, group_len
    )

    def query_part(lin_rows, gain_row):
        return query_rot(lin_rows, gain_row, angles, head_count)

    def key_part(lin_rows, gain_row):
        return key_rot(lin_rows, gain_row, angles)

    unused, pullback = jax.vjp(query_part, q_lin, head_gain[0])
    d_qlin, g_query = pullback(rotated_query_gradient)
    unused, pullback = jax.vjp(key_part, k_lin, head_gain[1])
    d_klin, g_key = pullback(d_packed[..., :head_width])
    d_query = d_qlin.astype(jnp.bfloat16)
    d_key = d_klin.astype(jnp.bfloat16)
    d_value = d_packed[..., head_width:].astype(jnp.bfloat16)
    dw_query = jnp.einsum("bce,bcd->ed", d_query, normed, preferred_element_type=jnp.float32)
    dw_key = jnp.einsum("bce,bcd->ed", d_key, normed, preferred_element_type=jnp.float32)
    dw_value = jnp.einsum("bce,bcd->ed", d_value, normed, preferred_element_type=jnp.float32)
    d_normed = (
        jnp.einsum("bce,ed->bcd", d_query, q_mat, preferred_element_type=jnp.float32)
        + jnp.einsum("bce,ed->bcd", d_key, k_mat, preferred_element_type=jnp.float32)
        + jnp.einsum("bce,ed->bcd", d_value, v_mat, preferred_element_type=jnp.float32)
    )
    unused, pullback = jax.vjp(norm_gain, stream, gains[0])
    d_stream, g_pre_attn = pullback(d_normed)
    d_stream = d_after + d_stream
    grads = (dw_query, dw_key, dw_value, dw_output, dw_gate, dw_up, dw_down)
    return (
        d_stream,
        grads,
        jnp.stack([g_pre_attn, g_post_attn, g_pre_ff, g_post_ff]),
        jnp.stack([g_query, g_key]),
    )


def body(
    tokens,
    group_offset,
    q_weight,
    k_weight,
    v_weight,
    o_weight,
    gate_weight,
    up_weight,
    down_weight,
    norm_gains,
    head_gains,
    out_grad,
):
    group_len = tokens.shape[1]
    layer_count = q_weight.shape[0]
    head_width = head_gains.shape[-1]
    hop_count = WINDOW // group_len
    position = group_offset + jnp.arange(group_len, dtype=jnp.int32)[None, :]
    angles = position.astype(jnp.float32)[..., None] * frequencies(head_width)[None, None, :]
    key_span = (hop_count + 1) * group_len
    distance = (
        jnp.arange(group_len, dtype=jnp.int32)[:, None]
        + hop_count * group_len
        - jnp.arange(key_span, dtype=jnp.int32)[None, :]
    )
    allowed = (
        (distance[None] >= 0) & (distance[None] < WINDOW) & (distance[None] <= position[:, :, None])
    )
    weights = (q_weight, k_weight, v_weight, o_weight, gate_weight, up_weight, down_weight)
    stream = tokens.astype(jnp.float32)
    records = []
    for layer_idx in range(layer_count):
        gathered = layer_weights(weights, layer_idx)
        saved, stream = forward_layer(
            stream,
            gathered,
            norm_gains[layer_idx],
            head_gains[layer_idx],
            angles,
            allowed,
            hop_count,
        )
        records.append((saved, None))
    block_out = stream.astype(jnp.bfloat16)
    upstream = out_grad.astype(jnp.float32)
    weight_shares = [None] * layer_count
    norm_parts = [None] * layer_count
    head_parts = [None] * layer_count
    for layer_idx in range(layer_count - 1, -1, -1):
        saved, kept_mats = records[layer_idx]
        gathered = layer_weights(weights, layer_idx)
        upstream, grads, norm_part, head_part = backward_layer(
            upstream,
            saved,
            gathered,
            norm_gains[layer_idx],
            head_gains[layer_idx],
            angles,
            allowed,
            hop_count,
        )
        weight_shares[layer_idx] = share_grads(grads)
        norm_parts[layer_idx] = norm_part
        head_parts[layer_idx] = head_part
    norm_total, head_total = lax.psum(
        (jnp.stack(norm_parts), jnp.stack(head_parts)), ("seq", "wsh")
    )
    stacked = tuple(
        (
            jnp.stack([weight_shares[layer_idx][member] for layer_idx in range(layer_count)])
            for member in range(7)
        )
    )
    return (block_out, upstream) + stacked + (norm_total, head_total)


def solution(mesh):
    in_specs = (
        P("wsh", "seq", None),
        P("wsh", "seq"),
        P(None, ("seq", "wsh"), None),
        P(None, ("seq", "wsh"), None),
        P(None, ("seq", "wsh"), None),
        P(None, ("seq", "wsh"), None),
        P(None, ("seq", "wsh"), None),
        P(None, ("seq", "wsh"), None),
        P(None, ("seq", "wsh"), None),
        P(),
        P(),
        P("wsh", "seq", None),
    )
    out_specs = (
        P("wsh", "seq", None),
        P("wsh", "seq", None),
        P(None, ("seq", "wsh"), None),
        P(None, ("seq", "wsh"), None),
        P(None, ("seq", "wsh"), None),
        P(None, ("seq", "wsh"), None),
        P(None, ("seq", "wsh"), None),
        P(None, ("seq", "wsh"), None),
        P(None, ("seq", "wsh"), None),
        P(),
        P(),
    )
    return jax.shard_map(body, mesh=mesh, in_specs=in_specs, out_specs=out_specs, check_vma=False)
```

profile of v0, /device:TPU:0, one launch (start us, length us, event | category | flops | bytes accessed | tf_op | source)
XLA Modules:
  0.0 1461.1 jit_solution(12689846133697198424)
XLA Ops:
  19.9 71.8 %all-gather.1 = bf16[1,256,640]{2,1,0:T(8,128)(2,1)S(1)} all-gather(bf16[1,8,640]{2,1,0:T(8,128)(2,1)S(1)} %get-tuple-element.89), channel_id=3, replica_groups=mesh['seq'=16,'wsh'=2] {'seq','wsh'}, dimensions={1}, use_global_device_ids=true | all-gather | bytes 337920 | tf_op jit(solution)/shard_map/all_gather | solution.py:58
  91.7 65.6 %all-gather = bf16[1,256,640]{2,1,0:T(8,128)(2,1)S(1)} all-gather(bf16[1,8,640]{2,1,0:T(8,128)(2,1)S(1)} %get-tuple-element.87), channel_id=2, replica_groups=mesh['seq'=16,'wsh'=2] {'seq','wsh'}, dimensions={1}, use_global_device_ids=true | all-gather | bytes 337920 | tf_op jit(solution)/shard_map/all_gather | solution.py:57
  171.0 13.7 collective-permute-start.2
  184.8 71.9 %all-gather.8 = bf16[1,256,640]{2,1,0:T(8,128)(2,1)} all-gather(bf16[1,8,640]{2,1,0:T(8,128)(2,1)S(1)} %get-tuple-element.88), channel_id=10, replica_groups=mesh['seq'=16,'wsh'=2] {'seq','wsh'}, dimensions={1}, use_global_device_ids=true | all-gather | bytes 337920 | tf_op jit(solution)/shard_map/all_gather | solution.py:58
  258.1 71.5 %all-gather.7 = bf16[1,256,640]{2,1,0:T(8,128)(2,1)} all-gather(bf16[1,8,640]{2,1,0:T(8,128)(2,1)S(1)} %get-tuple-element.86), channel_id=9, replica_groups=mesh['seq'=16,'wsh'=2] {'seq','wsh'}, dimensions={1}, use_global_device_ids=true | all-gather | bytes 337920 | tf_op jit(solution)/shard_map/all_gather | solution.py:57
  388.1 10.4 collective-permute-start.6
  432.1 56.1 %all-gather.39.cloned.1.call-done = bf16[1,2048,640]{2,1,0:T(8,128)(2,1)} async-done(((bf16[1,64,640]{2,1,0:T(8,128)(2,1)}), bf16[1,2048,640]{2,1,0:T(8,128)(2,1)}) %all-gather.39.cloned.1.call-update) | async-done | bytes 2621456 | tf_op jit(solution)/shard_map/all_gather | solution.py:60
  493.7 54.4 %all-gather.41.cloned.1.call-done = bf16[1,2048,640]{2,1,0:T(8,128)(2,1)} async-done(((bf16[1,64,640]{2,1,0:T(8,128)(2,1)}), bf16[1,2048,640]{2,1,0:T(8,128)(2,1)}) %all-gather.41.cloned.1.call-update) | async-done | bytes 2621456 | tf_op jit(solution)/shard_map/all_gather | solution.py:61
  554.4 53.4 %all-gather.43.cloned.1.call-done = bf16[1,2048,640]{2,1,0:T(8,128)(2,1)} async-done(((bf16[1,64,640]{2,1,0:T(8,128)(2,1)}), bf16[1,2048,640]{2,1,0:T(8,128)(2,1)}) %all-gather.43.cloned.1.call-update) | async-done | bytes 2621456 | tf_op jit(solution)/shard_map/all_gather | solution.py:62
  699.8 27.5 %all-to-all-start.2 = ((bf16[16,2,32,640]{3,2,1,0:T(8,128)(2,1)}), bf16[16,2,32,640]{3,2,1,0:T(8,128)(2,1)}, u32[]{:S(2)}, u32[]{:S(2)}) async-start(bf16[16,2,32,640]{3,2,1,0:T(8,128)(2,1)} %bitcast.411), calls=%async_computation.2 | async-start | bytes 2621440 | tf_op jit(solution)/shard_map/all_to_all | solution.py:77
  853.5 20.7 %all-to-all-start = ((bf16[16,2,32,640]{3,2,1,0:T(8,128)(2,1)}), bf16[16,2,32,640]{3,2,1,0:T(8,128)(2,1)}, u32[]{:S(2)}, u32[]{:S(2)}) async-start(bf16[16,2,32,640]{3,2,1,0:T(8,128)(2,1)} %bitcast.428), calls=%async_computation | async-start | bytes 2621440 | tf_op jit(solution)/shard_map/all_to_all | solution.py:77
  881.0 15.7 %collective-permute-done.15 = bf16[4,128,512]{2,1,0:T(8,128)(2,1)S(1)} collective-permute-done((bf16[4,128,512]{2,1,0:T(8,128)(2,1)S(1)}, bf16[4,128,512]{2,1,0:T(8,128)(2,1)S(1)}, u32[]{:S(2)}, u32[]{:S(2)}) %collective-permute-start.15) | collective-permute-done | bytes 524320 | tf_op jit(solution)/shard_map/ppermute | solution.py:17
  917.8 27.6 %all-to-all-start.8 = ((bf16[16,2,8,640]{3,2,1,0:T(8,128)(2,1)}), bf16[16,2,8,640]{3,2,1,0:T(8,128)(2,1)S(1)}, u32[]{:S(2)}, u32[]{:S(2)}) async-start(bf16[16,2,8,640]{3,2,1,0:T(8,128)(2,1)} %bitcast.81), calls=%async_computation.8 | async-start | bytes 655360 | tf_op jit(solution)/shard_map/all_to_all | solution.py:83
  995.8 45.1 %all-to-all-done.18 = bf16[16,2,64,640]{3,2,1,0:T(8,128)(2,1)S(1)} async-done(((bf16[16,2,64,640]{3,2,1,0:T(8,128)(2,1)}), bf16[16,2,64,640]{3,2,1,0:T(8,128)(2,1)S(1)}, u32[]{:S(2)}, u32[]{:S(2)}) %all-to-all-start.18) | async-done | bytes 2621472 | tf_op jit(solution)/shard_map/all_to_all | solution.py:89
  1040.9 13.3 all-to-all-start.22
  1059.4 45.2 %all-to-all-done.22 = bf16[16,2,64,640]{3,2,1,0:T(8,128)(2,1)} async-done(((bf16[16,2,64,640]{3,2,1,0:T(8,128)(2,1)}), bf16[16,2,64,640]{3,2,1,0:T(8,128)(2,1)}, u32[]{:S(2)}, u32[]{:S(2)}) %all-to-all-start.22) | async-done | bytes 2621472 | tf_op jit(solution)/shard_map/all_to_all | solution.py:92
  1104.6 13.4 all-to-all-start.26
  1119.0 49.2 %all-to-all-done.26 = bf16[16,2,64,640]{3,2,1,0:T(8,128)(2,1)} async-done(((bf16[16,2,64,640]{3,2,1,0:T(8,128)(2,1)}), bf16[16,2,64,640]{3,2,1,0:T(8,128)(2,1)}, u32[]{:S(2)}, u32[]{:S(2)}) %all-to-all-start.26) | async-done | bytes 2621472 | tf_op jit(solution)/shard_map/all_to_all | solution.py:95
  1195.2 12.9 all-to-all-start.24
  1213.2 45.1 %all-to-all-done.24 = bf16[16,2,64,640]{3,2,1,0:T(8,128)(2,1)S(1)} async-done(((bf16[16,2,64,640]{3,2,1,0:T(8,128)(2,1)}), bf16[16,2,64,640]{3,2,1,0:T(8,128)(2,1)S(1)}, u32[]{:S(2)}, u32[]{:S(2)}) %all-to-all-start.24) | async-done | bytes 2621472 | tf_op jit(solution)/shard_map/all_to_all | solution.py:95
  1259.9 13.3 all-to-all-start.16
  1278.2 45.2 %all-to-all-done.16 = bf16[16,2,64,640]{3,2,1,0:T(8,128)(2,1)S(1)} async-done(((bf16[16,2,64,640]{3,2,1,0:T(8,128)(2,1)}), bf16[16,2,64,640]{3,2,1,0:T(8,128)(2,1)S(1)}, u32[]{:S(2)}, u32[]{:S(2)}) %all-to-all-start.16) | async-done | bytes 2621472 | tf_op jit(solution)/shard_map/all_to_all | solution.py:89
  1324.9 13.4 all-to-all-start.20
  1351.1 68.5 %all-reduce.8 = (f32[2,4,640]{2,1,0:T(4,128)}, f32[2,2,256]{2,1,0:T(2,128)}) all-reduce(f32[2,4,640]{2,1,0:T(4,128)S(1)} %pad_maximum_fusion.11, f32[2,2,256]{2,1,0:T(2,128)S(1)} %pad_maximum_fusion.12), channel_id=1, replica_groups=mesh['seq'=16,'wsh'=2] {'seq','wsh'}, use_global_device_ids=true, to_apply=%region_66.67 | all-reduce | flops 6144 | bytes 49152 | tf_op jit(solution)/shard_map/psum | solution.py:390
  (707 shorter events, 518.6 us)
Async XLA Ops:
  7.2 326.9 %all-gather.25.cloned.1.call-start = ((), (), s32[]{:S(2)}) async-start(), calls=%async_computation.28 | async-start | bytes 1351680 | tf_op jit(solution)/shard_map/all_gather | solution.py:56
  8.8 343.4 %all-gather.27.cloned.1.call-start = ((), (), s32[]{:S(2)}) async-start(), calls=%async_computation.29 | async-start | bytes 1351680 | tf_op jit(solution)/shard_map/all_gather | solution.py:59
  10.3 346.4 %all-gather.29.cloned.1.call-start = ((), (), s32[]{:S(2)}) async-start(), calls=%async_computation.30 | async-start | bytes 2703360 | tf_op jit(solution)/shard_map/all_gather | solution.py:60
  12.0 350.7 %all-gather.31.cloned.1.call-start = ((), (), s32[]{:S(2)}) async-start(), calls=%async_computation.31 | async-start | bytes 2703360 | tf_op jit(solution)/shard_map/all_gather | solution.py:61
  13.7 355.3 %all-gather.33.cloned.1.call-start = ((), (), s32[]{:S(2)}) async-start(), calls=%async_computation.32 | async-start | bytes 2703360 | tf_op jit(solution)/shard_map/all_gather | solution.py:62
  15.3 383.2 %all-gather.35.cloned.1.call-start = ((), (), s32[]{:S(2)}) async-start(), calls=%async_computation.33 | async-start | bytes 1351680 | tf_op jit(solution)/shard_map/all_gather | solution.py:56
  15.9 411.7 %all-gather.37.cloned.1.call-start = ((), (), s32[]{:S(2)}) async-start(), calls=%async_computation.34 | async-start | bytes 1351680 | tf_op jit(solution)/shard_map/all_gather | solution.py:59
  16.7 471.5 %all-gather.39.cloned.1.call-start = ((), (), s32[]{:S(2)}) async-start(), calls=%async_computation.35 | async-start | bytes 2703360 | tf_op jit(solution)/shard_map/all_gather | solution.py:60
  17.4 530.7 %all-gather.41.cloned.1.call-start = ((), (), s32[]{:S(2)}) async-start(), calls=%async_computation.36 | async-start | bytes 2703360 | tf_op jit(solution)/shard_map/all_gather | solution.py:61
  171.0 85.8 %collective-permute-start.2 = (bf16[4,128,512]{2,1,0:T(8,128)(2,1)S(1)}, bf16[4,128,512]{2,1,0:T(8,128)(2,1)S(1)}, u32[]{:S(2)}, u32[]{:S(2)}) collective-permute-start(bf16[4,128,512]{2,1,0:T(8,128)(2,1)S(1)} %collective-permute-done.1), channel_id=1, source_target_pairs={{0,2},{2,4},{4,6},{6,8},{8,10},{10,12},{12,14},{14,16},{16,18},{18... | collective-permute-start | bytes 1572872 | tf_op jit(solution)/shard_map/ppermute | solution.py:17
  184.7 423.1 %all-gather.43.cloned.1.call-start = ((), (), s32[]{:S(2)}) async-start(), calls=%async_computation.37 | async-start | bytes 2703360 | tf_op jit(solution)/shard_map/all_gather | solution.py:62
  256.8 73.1 %collective-permute-start.3 = (bf16[4,128,512]{2,1,0:T(8,128)(2,1)S(1)}, bf16[4,128,512]{2,1,0:T(8,128)(2,1)S(1)}, u32[]{:S(2)}, u32[]{:S(2)}) collective-permute-start(bf16[4,128,512]{2,1,0:T(8,128)(2,1)S(1)} %collective-permute-done.2), channel_id=1, source_target_pairs={{0,2},{2,4},{4,6},{6,8},{8,10},{10,12},{12,14},{14,16},{16,18},{18... | collective-permute-start | bytes 1572872 | tf_op jit(solution)/shard_map/ppermute | solution.py:17
  646.7 53.0 %all-to-all-start.14 = ((bf16[16,2,32,640]{3,2,1,0:T(8,128)(2,1)}), bf16[16,2,32,640]{3,2,1,0:T(8,128)(2,1)}, u32[]{:S(2)}, u32[]{:S(2)}) async-start(bf16[16,2,32,640]{3,2,1,0:T(8,128)(2,1)} %bitcast.427), calls=%async_computation.14 | async-start | bytes 2621440 | tf_op jit(solution)/shard_map/all_to_all | solution.py:86
  699.8 55.0 %all-to-all-start.2 = ((bf16[16,2,32,640]{3,2,1,0:T(8,128)(2,1)}), bf16[16,2,32,640]{3,2,1,0:T(8,128)(2,1)}, u32[]{:S(2)}, u32[]{:S(2)}) async-start(bf16[16,2,32,640]{3,2,1,0:T(8,128)(2,1)} %bitcast.411), calls=%async_computation.2 | async-start | bytes 2621440 | tf_op jit(solution)/shard_map/all_to_all | solution.py:77
  821.7 31.8 %all-to-all-start.12 = ((bf16[16,2,32,640]{3,2,1,0:T(8,128)(2,1)}), bf16[16,2,32,640]{3,2,1,0:T(8,128)(2,1)}, u32[]{:S(2)}, u32[]{:S(2)}) async-start(bf16[16,2,32,640]{3,2,1,0:T(8,128)(2,1)} %bitcast.410), calls=%async_computation.12 | async-start | bytes 2621440 | tf_op jit(solution)/shard_map/all_to_all | solution.py:86
  843.0 31.2 %collective-permute-start.13 = (bf16[4,128,512]{2,1,0:T(8,128)(2,1)}, bf16[4,128,512]{2,1,0:T(8,128)(2,1)}, u32[]{:S(2)}, u32[]{:S(2)}) collective-permute-start(bf16[4,128,512]{2,1,0:T(8,128)(2,1)} %fusion.104), channel_id=1, source_target_pairs={{2,0},{4,2},{6,4},{8,6},{10,8},{12,10},{14,12},{16,14},{18,16},{20... | collective-permute-start | bytes 1572872 | tf_op jit(solution)/shard_map/ppermute | solution.py:17
  853.5 48.3 %all-to-all-start = ((bf16[16,2,32,640]{3,2,1,0:T(8,128)(2,1)}), bf16[16,2,32,640]{3,2,1,0:T(8,128)(2,1)}, u32[]{:S(2)}, u32[]{:S(2)}) async-start(bf16[16,2,32,640]{3,2,1,0:T(8,128)(2,1)} %bitcast.428), calls=%async_computation | async-start | bytes 2621440 | tf_op jit(solution)/shard_map/all_to_all | solution.py:77
  917.8 38.7 %all-to-all-start.8 = ((bf16[16,2,8,640]{3,2,1,0:T(8,128)(2,1)}), bf16[16,2,8,640]{3,2,1,0:T(8,128)(2,1)S(1)}, u32[]{:S(2)}, u32[]{:S(2)}) async-start(bf16[16,2,8,640]{3,2,1,0:T(8,128)(2,1)} %bitcast.81), calls=%async_computation.8 | async-start | bytes 655360 | tf_op jit(solution)/shard_map/all_to_all | solution.py:83
  987.0 53.9 %all-to-all-start.18 = ((bf16[16,2,64,640]{3,2,1,0:T(8,128)(2,1)}), bf16[16,2,64,640]{3,2,1,0:T(8,128)(2,1)S(1)}, u32[]{:S(2)}, u32[]{:S(2)}) async-start(bf16[16,2,64,640]{3,2,1,0:T(8,128)(2,1)} %bitcast.439), calls=%async_computation.18 | async-start | bytes 5242880 | tf_op jit(solution)/shard_map/all_to_all | solution.py:89
  1040.9 63.6 %all-to-all-start.22 = ((bf16[16,2,64,640]{3,2,1,0:T(8,128)(2,1)}), bf16[16,2,64,640]{3,2,1,0:T(8,128)(2,1)}, u32[]{:S(2)}, u32[]{:S(2)}) async-start(bf16[16,2,64,640]{3,2,1,0:T(8,128)(2,1)} %bitcast.438), calls=%async_computation.22 | async-start | bytes 5242880 | tf_op jit(solution)/shard_map/all_to_all | solution.py:92
  1104.6 63.7 %all-to-all-start.26 = ((bf16[16,2,64,640]{3,2,1,0:T(8,128)(2,1)}), bf16[16,2,64,640]{3,2,1,0:T(8,128)(2,1)}, u32[]{:S(2)}, u32[]{:S(2)}) async-start(bf16[16,2,64,640]{3,2,1,0:T(8,128)(2,1)} %bitcast.440), calls=%async_computation.26 | async-start | bytes 5242880 | tf_op jit(solution)/shard_map/all_to_all | solution.py:95
  1195.2 63.2 %all-to-all-start.24 = ((bf16[16,2,64,640]{3,2,1,0:T(8,128)(2,1)}), bf16[16,2,64,640]{3,2,1,0:T(8,128)(2,1)S(1)}, u32[]{:S(2)}, u32[]{:S(2)}) async-start(bf16[16,2,64,640]{3,2,1,0:T(8,128)(2,1)} %bitcast.441), calls=%async_computation.24 | async-start | bytes 5242880 | tf_op jit(solution)/shard_map/all_to_all | solution.py:95
  1259.9 63.6 %all-to-all-start.16 = ((bf16[16,2,64,640]{3,2,1,0:T(8,128)(2,1)}), bf16[16,2,64,640]{3,2,1,0:T(8,128)(2,1)S(1)}, u32[]{:S(2)}, u32[]{:S(2)}) async-start(bf16[16,2,64,640]{3,2,1,0:T(8,128)(2,1)} %bitcast.442), calls=%async_computation.16 | async-start | bytes 5242880 | tf_op jit(solution)/shard_map/all_to_all | solution.py:89
  1324.9 103.4 %all-to-all-start.20 = ((bf16[16,2,64,640]{3,2,1,0:T(8,128)(2,1)}), bf16[16,2,64,640]{3,2,1,0:T(8,128)(2,1)}, u32[]{:S(2)}, u32[]{:S(2)}) async-start(bf16[16,2,64,640]{3,2,1,0:T(8,128)(2,1)} %bitcast.437), calls=%async_computation.20 | async-start | bytes 5242880 | tf_op jit(solution)/shard_map/all_to_all | solution.py:92
  (225 other events, 4834.2 us)
Sparse Core Ops, SparseCore 0:
  11.5 57.6 all-gather.24
  72.0 53.1 all-gather.26
  128.7 60.4 all-gather.28
  192.5 58.3 all-gather.30
  253.7 57.2 all-gather.32
  314.3 53.3 all-gather.34
  370.6 57.0 all-gather.36
  431.1 56.9 all-gather.38
  491.1 56.9 all-gather.40
  550.8 56.9 all-gather.42
where the time goes:
time: 1470 us; the launch traced here: 1460 us
  waiting for transfers between devices  512 us (35%)
  blocking collectives  349 us (24%)
  starting transfers between devices  273 us (19%)
  matrix products  154 us (10%)
  other arithmetic  91 us (6%)
  local copies, waits for them, and re-layouts  64.6 us (4%)
  between operations  17.5 us (1%)
    all_gather x2, blocking collectives, layer_weights(): lax.all_gather(v_rows[layer_idx], ('seq', 'wsh'), axis=0, tiled=True)  144 us
    all_gather x2, blocking collectives, layer_weights(): lax.all_gather(k_rows[layer_idx], ('seq', 'wsh'), axis=0, tiled=True)  137 us
    all_to_all x2, waiting for transfers between devices, share_grads(): lax.all_to_all(dw_down.astype(jnp.bfloat16), 'seq', split_axis=0, concat_...  94.4 us
    all_to_all x2, waiting for transfers between devices, share_grads(): lax.all_to_all(dw_gate.astype(jnp.bfloat16), 'seq', split_axis=0, concat_...  90.3 us
    psum x1, blocking collectives, body(): lax.psum((jnp.stack(norm_parts), jnp.stack(head_parts)), ('seq', 'wsh'))  68.5 us
    all_gather x2, waiting for transfers between devices, layer_weights(): lax.all_gather(gate_rows[layer_idx], ('seq', 'wsh'), axis=0, tiled=True)  56.1 us
    all_gather x2, waiting for transfers between devices, layer_weights(): lax.all_gather(up_rows[layer_idx], ('seq', 'wsh'), axis=0, tiled=True)  54.4 us
    all_gather x2, waiting for transfers between devices, layer_weights(): lax.all_gather(down_rows[layer_idx], ('seq', 'wsh'), axis=0, tiled=True)  53.4 us
  transfers between devices with their start and end apart: 54, of which 36 were waited for; matrix products, arithmetic and copies ran while one was open for 17% of the time, Pallas kernels for 0%

commit v1 on v0

--- a/solution.py
+++ b/solution.py
@@ -25,8 +25,7 @@
     half_width = values.shape[-1] // 2
     leading = values[..., :half_width]
     trailing = values[..., half_width:]
-    cosine = jnp.cos(angles)
-    sine_part = jnp.sin(angles)
+    cosine, sine_part = angles
     return jnp.concatenate(
         [leading * cosine - trailing * sine_part, trailing * cosine + leading * sine_part], axis=-1
     )
@@ -43,109 +42,174 @@
 
 def query_rot(q_lin, head_gain, angles, head_count):
     shaped = q_lin.reshape(q_lin.shape[0], q_lin.shape[1], head_count, -1)
-    return rotate(norm_gain(shaped, head_gain), angles[:, :, None, :]) * shaped.shape[-1] ** (-0.5)
+    return rotate(
+        norm_gain(shaped, head_gain), tuple(part[:, :, None, :] for part in angles)
+    ) * shaped.shape[-1] ** (-0.5)
 
 
 def key_rot(k_lin, head_gain, angles):
     return rotate(norm_gain(k_lin, head_gain), angles)
 
 
+def device_index():
+    return lax.axis_index("seq") * lax.axis_size("wsh") + lax.axis_index("wsh")
+
+
+def bits_of(size, unit):
+    found = []
+    step = 1
+    while step < size:
+        found.insert(0, step * unit)
+        step *= 2
+    return found
+
+
+def exchange_plan():
+    wsh_count = lax.axis_size("wsh")
+    seq_bits = bits_of(lax.axis_size("seq"), wsh_count)
+    wsh_bits = bits_of(wsh_count, 1)
+    core_bit = seq_bits[-1]
+    near_bit = seq_bits[-2:-1]
+    far_bits = seq_bits[:-2]
+    orders = (far_bits + wsh_bits + near_bit, near_bit + far_bits + wsh_bits)
+    return core_bit, orders, far_bits + near_bit, wsh_bits
+
+
+def flip(value, bit_of_core):
+    core_bit = exchange_plan()[0]
+    count = lax.axis_size("seq") * lax.axis_size("wsh")
+    pairs = [(d, d ^ bit_of_core[1 if d & core_bit else 0]) for d in range(count)]
+    return lax.ppermute(value, ("seq", "wsh"), pairs)
+
+
+def my_bit(bit_of_core):
+    me = device_index()
+    core = (me & exchange_plan()[0]) != 0
+    return jnp.where(core, me & bit_of_core[1], me & bit_of_core[0]) != 0
+
+
+def is_upper_core():
+    return (device_index() & exchange_plan()[0]) != 0
+
+
+def gather_blocks(block, ordered, axis):
+    core_bit, orders, upper_bits, wsh_bits = exchange_plan()
+    held = jnp.expand_dims(block, axis)
+    for pair in zip(*orders):
+        came = flip(held, pair)
+        if ordered:
+            swap = my_bit(pair)
+            held = jnp.concatenate(
+                [jnp.where(swap, came, held), jnp.where(swap, held, came)], axis=axis
+            )
+        else:
+            held = jnp.concatenate([held, came], axis=axis)
+    came = flip(held, (core_bit, core_bit))
+    if not ordered:
+        return jnp.concatenate([held, came], axis=axis)
+    upper = is_upper_core()
+    halves = (jnp.where(upper, came, held), jnp.where(upper, held, came))
+    target = upper_bits + wsh_bits
+    placed = []
+    for half, order in zip(halves, orders):
+        split = half.reshape((2,) * len(order) + half.shape[1:])
+        stored = order[::-1]
+        trailing = tuple(range(len(order), split.ndim))
+        placed.append(split.transpose(tuple(stored.index(bit) for bit in target) + trailing))
+    whole = jnp.stack(placed, axis=len(upper_bits))
+    return whole.reshape((-1,) + block.shape)
+
+
+def add_terms(kept, came):
+    return kept.astype(jnp.float32) + came.astype(jnp.float32)
+
+
+def scatter_blocks(blocks, ordered, axis):
+    core_bit, orders, upper_bits, wsh_bits = exchange_plan()
+    if ordered:
+        target = upper_bits + wsh_bits
+        split = blocks.reshape((2,) * (len(target) + 1) + blocks.shape[1:])
+        parts = []
+        for core, order in enumerate(orders):
+            half = lax.index_in_dim(split, core, len(upper_bits), keepdims=False)
+            trailing = tuple(range(len(order), half.ndim))
+            half = half.transpose(tuple(target.index(bit) for bit in order[::-1]) + trailing)
+            parts.append(half.reshape((-1,) + blocks.shape[1:]))
+        upper = is_upper_core()
+        kept = jnp.where(upper, parts[1], parts[0])
+        sent = jnp.where(upper, parts[0], parts[1])
+    else:
+        kept, sent = jnp.split(blocks, 2, axis=axis)
+    total = add_terms(kept, flip(sent, (core_bit, core_bit)))
+    for pair in list(zip(*orders))[::-1]:
+        total = total.astype(jnp.bfloat16)
+        kept, sent = jnp.split(total, 2, axis=axis)
+        if ordered:
+            swap = my_bit(pair)
+            kept, sent = (jnp.where(swap, sent, kept), jnp.where(swap, kept, sent))
+        total = add_terms(kept, flip(sent, pair))
+    return jnp.squeeze(total, axis)
+
+
+def sum_all(value):
+    core_bit, orders, upper_bits, wsh_bits = exchange_plan()
+    for bit in [core_bit] + upper_bits[::-1] + wsh_bits:
+        value = value + flip(value, (bit, bit))
+    return value
+
+
 def layer_weights(weights, layer_idx):
-    q_rows, k_rows, v_rows, o_rows, gate_rows, up_rows, down_rows = weights
-    return (
-        lax.all_gather(q_rows[layer_idx], ("seq", "wsh"), axis=0, tiled=True),
-        lax.all_gather(k_rows[layer_idx], ("seq", "wsh"), axis=0, tiled=True),
-        lax.all_gather(v_rows[layer_idx], ("seq", "wsh"), axis=0, tiled=True),
-        lax.all_gather(o_rows[layer_idx], ("seq", "wsh"), axis=0, tiled=True),
-        lax.all_gather(gate_rows[layer_idx], ("seq", "wsh"), axis=0, tiled=True),
-        lax.all_gather(up_rows[layer_idx], ("seq", "wsh"), axis=0, tiled=True),
-        lax.all_gather(down_rows[layer_idx], ("seq", "wsh"), axis=0, tiled=True),
-    )
+    rows = [member[layer_idx] for member in weights]
+    attn = gather_blocks(jnp.concatenate(rows[:4], axis=0), True, 0)
+    ffn = gather_blocks(jnp.stack(rows[4:]), False, 1)
+    mats = []
+    start = 0
+    for member in rows[:4]:
+        mats.append(attn[:, start : start + member.shape[0]].reshape(-1, member.shape[1]))
+        start += member.shape[0]
+    for kind in range(3):
+        mats.append(ffn[kind].reshape(-1, ffn.shape[-1]))
+    return tuple(mats)
+
+
+def share_attn(grads):
+    count = lax.axis_size("seq") * lax.axis_size("wsh")
+    shaped = [
+        member.astype(jnp.bfloat16).reshape(count, -1, member.shape[1]) for member in grads
+    ]
+    summed = scatter_blocks(jnp.concatenate(shaped, axis=1), True, 0)
+    shares = []
+    start = 0
+    for member in shaped:
+        shares.append(summed[start : start + member.shape[1]])
+        start += member.shape[1]
+    return shares
+
+
+def share_ffn(grads):
+    count = lax.axis_size("seq") * lax.axis_size("wsh")
+    stacked = jnp.stack(
+        [member.astype(jnp.bfloat16).reshape(count, -1, member.shape[1]) for member in grads]
+    )
+    summed = scatter_blocks(stacked, False, 1)
+    return [summed[kind] for kind in range(3)]
 
 
 def share_grads(grads):
-    seq_count = lax.axis_size("seq")
-    wsh_count = lax.axis_size("wsh")
-    shaped = [
-        member.reshape(
-            seq_count, wsh_count, member.shape[0] // (seq_count * wsh_count), member.shape[1]
-        )
-        for member in grads
-    ]
-    dw_query, dw_key, dw_value, dw_output, dw_gate, dw_up, dw_down = shaped
-    moved = (
-        lax.all_to_all(
-            dw_query.astype(jnp.bfloat16), "seq", split_axis=0, concat_axis=0, tiled=True
-        ).astype(dw_query.dtype),
-        lax.all_to_all(
-            dw_key.astype(jnp.bfloat16), "seq", split_axis=0, concat_axis=0, tiled=True
-        ).astype(dw_key.dtype),
-        lax.all_to_all(
-            dw_value.astype(jnp.bfloat16), "seq", split_axis=0, concat_axis=0, tiled=True
-        ).astype(dw_value.dtype),
-        lax.all_to_all(
-            dw_output.astype(jnp.bfloat16), "seq", split_axis=0, concat_axis=0, tiled=True
-        ).astype(dw_output.dtype),
-        lax.all_to_all(
-            dw_gate.astype(jnp.bfloat16), "seq", split_axis=0, concat_axis=0, tiled=True
-        ).astype(dw_gate.dtype),
-        lax.all_to_all(
-            dw_up.astype(jnp.bfloat16), "seq", split_axis=0, concat_axis=0, tiled=True
-        ).astype(dw_up.dtype),
-        lax.all_to_all(
-            dw_down.astype(jnp.bfloat16), "seq", split_axis=0, concat_axis=0, tiled=True
-        ).astype(dw_down.dtype),
-    )
-    dw_query, dw_key, dw_value, dw_output, dw_gate, dw_up, dw_down = [
-        jnp.sum(member, axis=0) for member in moved
-    ]
-    moved = (
-        lax.all_to_all(
-            dw_query.astype(jnp.bfloat16), "wsh", split_axis=0, concat_axis=0, tiled=True
-        ).astype(dw_query.dtype),
-        lax.all_to_all(
-            dw_key.astype(jnp.bfloat16), "wsh", split_axis=0, concat_axis=0, tiled=True
-        ).astype(dw_key.dtype),
-        lax.all_to_all(
-            dw_value.astype(jnp.bfloat16), "wsh", split_axis=0, concat_axis=0, tiled=True
-        ).astype(dw_value.dtype),
-        lax.all_to_all(
-            dw_output.astype(jnp.bfloat16), "wsh", split_axis=0, concat_axis=0, tiled=True
-        ).astype(dw_output.dtype),
-        lax.all_to_all(
-            dw_gate.astype(jnp.bfloat16), "wsh", split_axis=0, concat_axis=0, tiled=True
-        ).astype(dw_gate.dtype),
-        lax.all_to_all(
-            dw_up.astype(jnp.bfloat16), "wsh", split_axis=0, concat_axis=0, tiled=True
-        ).astype(dw_up.dtype),
-        lax.all_to_all(
-            dw_down.astype(jnp.bfloat16), "wsh", split_axis=0, concat_axis=0, tiled=True
-        ).astype(dw_down.dtype),
-    )
-    return tuple((jnp.sum(member, axis=0) for member in moved))
+    return tuple(share_attn(grads[:4]) + share_ffn(grads[4:]))
 
 
 def earlier_keys(packed_tokens, hop_count):
-    pieces = []
-    moving = packed_tokens
-    for hop_idx in range(hop_count):
-        moving = shifted(moving, "seq", 1)
-        pieces.insert(0, moving)
+    pieces = [shifted(packed_tokens, "seq", hop) for hop in range(hop_count, 0, -1)]
     return jnp.concatenate(pieces + [packed_tokens], axis=1)
 
 
 def returned_grads(grad_all, hop_count, group_len):
-    slices = [
-        grad_all[:, (hop_count - hop_idx) * group_len : (hop_count - hop_idx + 1) * group_len]
-        for hop_idx in range(hop_count + 1)
-    ]
-    summed = slices[0]
-    moving = slices[hop_count]
-    for hop_idx in range(hop_count, 0, -1):
-        moving = shifted(moving.astype(jnp.bfloat16), "seq", -1).astype(moving.dtype)
-        if hop_idx > 1:
-            moving = moving + slices[hop_idx - 1]
-    summed = summed + moving
+    summed = grad_all[:, hop_count * group_len :]
+    for hop in range(hop_count, 0, -1):
+        start = (hop_count - hop) * group_len
+        piece = grad_all[:, start : start + group_len].astype(jnp.bfloat16)
+        summed = summed + shifted(piece, "seq", -hop).astype(jnp.float32)
     return summed
 
 
@@ -342,6 +406,7 @@
     hop_count = WINDOW // group_len
     position = group_offset + jnp.arange(group_len, dtype=jnp.int32)[None, :]
     angles = position.astype(jnp.float32)[..., None] * frequencies(head_width)[None, None, :]
+    angles = lax.optimization_barrier((jnp.cos(angles), jnp.sin(angles)))
     key_span = (hop_count + 1) * group_len
     distance = (
         jnp.arange(group_len, dtype=jnp.int32)[:, None]
@@ -365,7 +430,7 @@
             allowed,
             hop_count,
         )
-        records.append((saved, None))
+        records.append((saved, gathered))
     block_out = stream.astype(jnp.bfloat16)
     upstream = out_grad.astype(jnp.float32)
     weight_shares = [None] * layer_count
@@ -373,7 +438,7 @@
     head_parts = [None] * layer_count
     for layer_idx in range(layer_count - 1, -1, -1):
         saved, kept_mats = records[layer_idx]
-        gathered = layer_weights(weights, layer_idx)
+        gathered = kept_mats
         upstream, grads, norm_part, head_part = backward_layer(
             upstream,
             saved,
@@ -387,9 +452,16 @@
         weight_shares[layer_idx] = share_grads(grads)
         norm_parts[layer_idx] = norm_part
         head_parts[layer_idx] = head_part
-    norm_total, head_total = lax.psum(
-        (jnp.stack(norm_parts), jnp.stack(head_parts)), ("seq", "wsh")
-    )
+    totals = [None] * layer_count
+    for layer_idx in range(layer_count - 1, -1, -1):
+        flat = jnp.concatenate(
+            [norm_parts[layer_idx].reshape(-1), head_parts[layer_idx].reshape(-1)]
+        )
+        totals[layer_idx] = sum_all(flat.reshape(-1, 128))
+    both = jnp.stack(totals).reshape(layer_count, -1)
+    norm_size = norm_gains[0].size
+    norm_total = both[:, :norm_size].reshape(norm_gains.shape)
+    head_total = both[:, norm_size:].reshape(head_gains.shape)
     stacked = tuple(
         (
             jnp.stack([weight_shares[layer_idx][member] for layer_idx in range(layer_count)])

time: 1470 us -> 632 us (0.43)
  the two profiles are of different devices: /device:TPU:0 before, /device:TPU:1 now
where the time goes in v1:
time: 632 us; the launch traced here: 624 us
  waiting for transfers between devices  197 us (31%)
  starting transfers between devices  149 us (24%)
  matrix products  111 us (18%)
  other arithmetic  84.2 us (13%)
  local copies, waits for them, and re-layouts  78 us (12%)
    ppermute x50, waiting for transfers between devices, flip(): return lax.ppermute(value, ('seq', 'wsh'), pairs)  171 us
    ppermute x50, starting transfers between devices, flip(): return lax.ppermute(value, ('seq', 'wsh'), pairs)  81.9 us
    ppermute x16, starting transfers between devices, shifted(): lax.ppermute(value, axis, [(source, source + steps) for source in range(i...  67.5 us
    unnamed x322, local copies, waits for them, and re-layouts  37.2 us
    ppermute x16, waiting for transfers between devices, shifted(): lax.ppermute(value, axis, [(source, source + steps) for source in range(i...  26.6 us
    convert_element_type x16, other arithmetic, scatter_blocks(): total = total.astype(jnp.bfloat16)  18.9 us
  transfers between devices with their start and end apart: 66, of which 25 were waited for; matrix products, arithmetic and copies ran while one was open for 23% of the time, Pallas kernels for 0%

profile of v1, /device:TPU:1, one launch (start us, length us, event | category | flops | bytes accessed | tf_op | source)
XLA Modules:
  0.0 623.5 jit_solution(16647969737376202826)
XLA Ops:
  20.8 8.4 %collective-permute-done.1 = bf16[2,80,640]{2,1,0:T(8,128)(2,1)S(1)} collective-permute-done((bf16[2,80,640]{2,1,0:T(8,128)(2,1)S(1)}, bf16[2,80,640]{2,1,0:T(8,128)(2,1)S(1)}, u32[]{:S(2)}, u32[]{:S(2)}) %collective-permute-start.1) | collective-permute-done | bytes 204832 | tf_op jit(solution)/shard_map/ppermute | solution.py:82
  44.0 6.1 collective-permute-done.16
  52.6 7.2 %collective-permute-done.24 = bf16[3,2,64,640]{3,2,0,1:T(8,128)(2,1)S(1)} collective-permute-done((bf16[3,2,64,640]{3,2,0,1:T(8,128)(2,1)S(1)}, bf16[3,2,64,640]{3,2,0,1:T(8,128)(2,1)S(1)}, u32[]{:S(2)}, u32[]{:S(2)}) %collective-permute-start.24) | collective-permute-done | bytes 491552 | tf_op jit(solution)/shard_map/ppermute | solution.py:82
  61.1 16.5 %collective-permute-start.4 = (bf16[16,80,640]{2,1,0:T(8,128)(2,1)S(1)}, bf16[16,80,640]{2,1,0:T(8,128)(2,1)S(1)}, u32[]{:S(2)}, u32[]{:S(2)}) collective-permute-start(bf16[16,80,640]{2,1,0:T(8,128)(2,1)S(1)} %pad_maximum_fusion.10), channel_id=1, source_target_pairs={{0,2},{1,3},{2,0},{3,1},{4,6},{5,7},{6,4},{7,5},{8,10},{9,11},{10,... | collective-permute-start | bytes 4915208 | tf_op jit(solution)/shard_map/ppermute | solution.py:82
  82.1 9.8 %collective-permute-start.18 = (bf16[16,80,640]{2,1,0:T(8,128)(2,1)}, bf16[16,80,640]{2,1,0:T(8,128)(2,1)}, u32[]{:S(2)}, u32[]{:S(2)}) collective-permute-start(bf16[16,80,640]{2,1,0:T(8,128)(2,1)} %pad_maximum_fusion.11), channel_id=1, source_target_pairs={{0,2},{1,3},{2,0},{3,1},{4,6},{5,7},{6,4},{7,5},{8,10},{9,11},{10,... | collective-permute-start | bytes 4915208 | tf_op jit(solution)/shard_map/ppermute | solution.py:82
  106.5 14.3 %collective-permute-start.6 = (bf16[4,128,512]{2,1,0:T(8,128)(2,1)S(1)}, bf16[4,128,512]{2,1,0:T(8,128)(2,1)}, u32[]{:S(2)}, u32[]{:S(2)}) collective-permute-start(bf16[4,128,512]{2,1,0:T(8,128)(2,1)S(1)} %pad_maximum_fusion.16), channel_id=1, source_target_pairs={{0,6},{2,8},{4,10},{6,12},{8,14},{10,16},{12,18},{14,20},{16,22},{... | collective-permute-start | bytes 1572872 | tf_op jit(solution)/shard_map/ppermute | solution.py:17
  131.3 11.3 %collective-permute-done.12 = bf16[3,8,64,640]{3,2,0,1:T(8,128)(2,1)} collective-permute-done((bf16[3,8,64,640]{3,2,0,1:T(8,128)(2,1)}, bf16[3,8,64,640]{3,2,0,1:T(8,128)(2,1)}, u32[]{:S(2)}, u32[]{:S(2)}) %collective-permute-start.12) | collective-permute-done | bytes 1966112 | tf_op jit(solution)/shard_map/ppermute | solution.py:82
  187.2 9.5 %collective-permute-start.19 = (bf16[4,128,512]{2,1,0:T(8,128)(2,1)S(1)}, bf16[4,128,512]{2,1,0:T(8,128)(2,1)S(1)}, u32[]{:S(2)}, u32[]{:S(2)}) collective-permute-start(bf16[4,128,512]{2,1,0:T(8,128)(2,1)S(1)} %pad_maximum_fusion.17), channel_id=1, source_target_pairs={{0,8},{2,10},{4,12},{6,14},{8,16},{10,18},{12,20},{14,22},{16,24},... | collective-permute-start | bytes 1572872 | tf_op jit(solution)/shard_map/ppermute | solution.py:17
  196.7 17.3 %collective-permute-start.20 = (bf16[4,128,512]{2,1,0:T(8,128)(2,1)S(1)}, bf16[4,128,512]{2,1,0:T(8,128)(2,1)S(1)}, u32[]{:S(2)}, u32[]{:S(2)}) collective-permute-start(bf16[4,128,512]{2,1,0:T(8,128)(2,1)S(1)} %pad_maximum_fusion.17), channel_id=1, source_target_pairs={{0,6},{2,8},{4,10},{6,12},{8,14},{10,16},{12,18},{14,20},{16,22},{... | collective-permute-start | bytes 1572872 | tf_op jit(solution)/shard_map/ppermute | solution.py:17
  226.1 5.6 collective-permute-done.22
  310.8 14.2 %collective-permute-done.29 = bf16[4,128,512]{2,1,0:T(8,128)(2,1)} collective-permute-done((bf16[4,128,512]{2,1,0:T(8,128)(2,1)}, bf16[4,128,512]{2,1,0:T(8,128)(2,1)}, u32[]{:S(2)}, u32[]{:S(2)}) %collective-permute-start.29) | collective-permute-done | bytes 524320 | tf_op jit(solution)/shard_map/ppermute | solution.py:17
  351.2 5.3 convolution_bitcast_fusion
  395.6 13.2 %collective-permute-start.62 = (f32[24,128]{1,0:T(8,128)S(1)}, f32[24,128]{1,0:T(8,128)S(1)}, u32[]{:S(2)}, u32[]{:S(2)}) collective-permute-start(f32[24,128]{1,0:T(8,128)S(1)} %fusion.211), channel_id=1, source_target_pairs={{0,4},{1,5},{2,6},{3,7},{4,0},{5,1},{6,2},{7,3},{8,12},{9,13},{10,... | collective-permute-start | bytes 36872 | tf_op jit(solution)/shard_map/ppermute | solution.py:82
  411.6 5.4 collective-permute-done.62
  421.5 6.0 collective-permute-done.63
  434.1 7.1 %collective-permute-start.51 = (bf16[3,16,64,640]{3,2,1,0:T(8,128)(2,1)}, bf16[3,16,64,640]{3,2,1,0:T(8,128)(2,1)}, u32[]{:S(2)}, u32[]{:S(2)}) collective-permute-start(bf16[3,16,64,640]{3,2,1,0:T(8,128)(2,1)} %split.211), channel_id=1, source_target_pairs={{0,2},{1,3},{2,0},{3,1},{4,6},{5,7},{6,4},{7,5},{8,10},{9,11},{10,... | collective-permute-start | bytes 11796488 | tf_op jit(solution)/shard_map/ppermute | solution.py:82
  494.0 8.7 %collective-permute-done.37 = bf16[8,80,640]{2,1,0:T(8,128)(2,1)S(1)} collective-permute-done((bf16[8,80,640]{2,1,0:T(8,128)(2,1)}, bf16[8,80,640]{2,1,0:T(8,128)(2,1)S(1)}, u32[]{:S(2)}, u32[]{:S(2)}) %collective-permute-start.37) | collective-permute-done | bytes 819232 | tf_op jit(solution)/shard_map/ppermute | solution.py:82
  505.1 5.3 add_convert_fusion
  517.1 6.6 %collective-permute-done.39 = bf16[2,80,640]{2,1,0:T(8,128)(2,1)S(1)} collective-permute-done((bf16[2,80,640]{2,1,0:T(8,128)(2,1)S(1)}, bf16[2,80,640]{2,1,0:T(8,128)(2,1)S(1)}, u32[]{:S(2)}, u32[]{:S(2)}) %collective-permute-start.39) | collective-permute-done | bytes 204832 | tf_op jit(solution)/shard_map/ppermute | solution.py:82
  524.0 10.4 %collective-permute-done.52 = bf16[3,8,64,640]{3,2,1,0:T(8,128)(2,1)S(1)} collective-permute-done((bf16[3,8,64,640]{3,2,1,0:T(8,128)(2,1)S(1)}, bf16[3,8,64,640]{3,2,1,0:T(8,128)(2,1)S(1)}, u32[]{:S(2)}, u32[]{:S(2)}) %collective-permute-start.52) | collective-permute-done | bytes 1966112 | tf_op jit(solution)/shard_map/ppermute | solution.py:82
  535.3 30.4 %collective-permute-done.47 = bf16[3,8,64,640]{3,2,1,0:T(8,128)(2,1)S(1)} collective-permute-done((bf16[3,8,64,640]{3,2,1,0:T(8,128)(2,1)S(1)}, bf16[3,8,64,640]{3,2,1,0:T(8,128)(2,1)S(1)}, u32[]{:S(2)}, u32[]{:S(2)}) %collective-permute-start.47) | collective-permute-done | bytes 1966112 | tf_op jit(solution)/shard_map/ppermute | solution.py:82
  568.3 27.6 %collective-permute-done.48 = bf16[3,4,64,640]{3,2,1,0:T(8,128)(2,1)S(1)} collective-permute-done((bf16[3,4,64,640]{3,2,1,0:T(8,128)(2,1)S(1)}, bf16[3,4,64,640]{3,2,1,0:T(8,128)(2,1)S(1)}, u32[]{:S(2)}, u32[]{:S(2)}) %collective-permute-start.48) | collective-permute-done | bytes 983072 | tf_op jit(solution)/shard_map/ppermute | solution.py:82
  598.5 17.2 %collective-permute-done.49 = bf16[3,2,64,640]{3,2,1,0:T(8,128)(2,1)S(1)} collective-permute-done((bf16[3,2,64,640]{3,2,1,0:T(8,128)(2,1)S(1)}, bf16[3,2,64,640]{3,2,1,0:T(8,128)(2,1)S(1)}, u32[]{:S(2)}, u32[]{:S(2)}) %collective-permute-start.49) | collective-permute-done | bytes 491552 | tf_op jit(solution)/shard_map/ppermute | solution.py:82
  616.1 4.9 collective-permute-done.50
  (717 shorter events, 351.6 us)
Async XLA Ops:
  3.6 36.9 %collective-permute-start.23 = (bf16[3,1,64,640]{3,2,0,1:T(8,128)(2,1)S(1)}, bf16[3,1,64,640]{3,2,0,1:T(8,128)(2,1)S(1)}, u32[]{:S(2)}, u32[]{:S(2)}) collective-permute-start(bf16[3,1,64,640]{3,2,0,1:T(8,128)(2,1)S(1)} %maximum_bitcast_fusion.1), channel_id=1, source_target_pairs={{0,16},{1,17},{2,6},{3,7},{4,20},{5,21},{6,2},{7,3},{8,24},{9,25},... | collective-permute-start | bytes 737288 | tf_op jit(solution)/shard_map/ppermute | solution.py:82
  8.1 34.9 %collective-permute-start.9 = (bf16[3,1,64,640]{3,2,0,1:T(8,128)(2,1)S(1)}, bf16[3,1,64,640]{3,2,0,1:T(8,128)(2,1)S(1)}, u32[]{:S(2)}, u32[]{:S(2)}) collective-permute-start(bf16[3,1,64,640]{3,2,0,1:T(8,128)(2,1)S(1)} %maximum_bitcast_fusion), channel_id=1, source_target_pairs={{0,16},{1,17},{2,6},{3,7},{4,20},{5,21},{6,2},{7,3},{8,24},{9,25},... | collective-permute-start | bytes 737288 | tf_op jit(solution)/shard_map/ppermute | solution.py:82
  43.0 34.5 %collective-permute-start.10 = (bf16[3,2,64,640]{3,2,0,1:T(8,128)(2,1)S(1)}, bf16[3,2,64,640]{3,2,0,1:T(8,128)(2,1)S(1)}, u32[]{:S(2)}, u32[]{:S(2)}) collective-permute-start(bf16[3,2,64,640]{3,2,0,1:T(8,128)(2,1)S(1)} %pad_maximum_fusion.18), channel_id=1, source_target_pairs={{0,8},{1,9},{2,18},{3,19},{4,12},{5,13},{6,22},{7,23},{8,0},{9,1},... | collective-permute-start | bytes 1474568 | tf_op jit(solution)/shard_map/ppermute | solution.py:82
  60.0 32.0 %collective-permute-start.25 = (bf16[3,4,64,640]{3,2,0,1:T(8,128)(2,1)S(1)}, bf16[3,4,64,640]{3,2,0,1:T(8,128)(2,1)S(1)}, u32[]{:S(2)}, u32[]{:S(2)}) collective-permute-start(bf16[3,4,64,640]{3,2,0,1:T(8,128)(2,1)S(1)} %pad_maximum_fusion.13), channel_id=1, source_target_pairs={{0,1},{1,0},{2,10},{3,11},{4,5},{5,4},{6,14},{7,15},{8,9},{9,8},{1... | collective-permute-start | bytes 2949128 | tf_op jit(solution)/shard_map/ppermute | solution.py:82
  61.1 40.2 %collective-permute-start.4 = (bf16[16,80,640]{2,1,0:T(8,128)(2,1)S(1)}, bf16[16,80,640]{2,1,0:T(8,128)(2,1)S(1)}, u32[]{:S(2)}, u32[]{:S(2)}) collective-permute-start(bf16[16,80,640]{2,1,0:T(8,128)(2,1)S(1)} %pad_maximum_fusion.10), channel_id=1, source_target_pairs={{0,2},{1,3},{2,0},{3,1},{4,6},{5,7},{6,4},{7,5},{8,10},{9,11},{10,... | collective-permute-start | bytes 4915208 | tf_op jit(solution)/shard_map/ppermute | solution.py:82
  82.1 38.7 %collective-permute-start.18 = (bf16[16,80,640]{2,1,0:T(8,128)(2,1)}, bf16[16,80,640]{2,1,0:T(8,128)(2,1)}, u32[]{:S(2)}, u32[]{:S(2)}) collective-permute-start(bf16[16,80,640]{2,1,0:T(8,128)(2,1)} %pad_maximum_fusion.11), channel_id=1, source_target_pairs={{0,2},{1,3},{2,0},{3,1},{4,6},{5,7},{6,4},{7,5},{8,10},{9,11},{10,... | collective-permute-start | bytes 4915208 | tf_op jit(solution)/shard_map/ppermute | solution.py:82
  92.2 54.1 %collective-permute-start.26 = (bf16[3,8,64,640]{3,2,0,1:T(8,128)(2,1)S(1)}, bf16[3,8,64,640]{3,2,0,1:T(8,128)(2,1)S(1)}, u32[]{:S(2)}, u32[]{:S(2)}) collective-permute-start(bf16[3,8,64,640]{3,2,0,1:T(8,128)(2,1)S(1)} %pad_maximum_fusion.9), channel_id=1, source_target_pairs={{0,4},{1,5},{2,3},{3,2},{4,0},{5,1},{6,7},{7,6},{8,12},{9,13},{10,... | collective-permute-start | bytes 5898248 | tf_op jit(solution)/shard_map/ppermute | solution.py:82
  98.5 44.1 %collective-permute-start.12 = (bf16[3,8,64,640]{3,2,0,1:T(8,128)(2,1)}, bf16[3,8,64,640]{3,2,0,1:T(8,128)(2,1)}, u32[]{:S(2)}, u32[]{:S(2)}) collective-permute-start(bf16[3,8,64,640]{3,2,0,1:T(8,128)(2,1)} %pad_maximum_fusion.8), channel_id=1, source_target_pairs={{0,4},{1,5},{2,3},{3,2},{4,0},{5,1},{6,7},{7,6},{8,12},{9,13},{10,... | collective-permute-start | bytes 5898248 | tf_op jit(solution)/shard_map/ppermute | solution.py:82
  104.4 47.3 %collective-permute-start.5 = (bf16[4,128,512]{2,1,0:T(8,128)(2,1)S(1)}, bf16[4,128,512]{2,1,0:T(8,128)(2,1)}, u32[]{:S(2)}, u32[]{:S(2)}) collective-permute-start(bf16[4,128,512]{2,1,0:T(8,128)(2,1)S(1)} %pad_maximum_fusion.16), channel_id=1, source_target_pairs={{0,8},{2,10},{4,12},{6,14},{8,16},{10,18},{12,20},{14,22},{16,24},... | collective-permute-start | bytes 1572872 | tf_op jit(solution)/shard_map/ppermute | solution.py:17
  106.5 46.2 %collective-permute-start.6 = (bf16[4,128,512]{2,1,0:T(8,128)(2,1)S(1)}, bf16[4,128,512]{2,1,0:T(8,128)(2,1)}, u32[]{:S(2)}, u32[]{:S(2)}) collective-permute-start(bf16[4,128,512]{2,1,0:T(8,128)(2,1)S(1)} %pad_maximum_fusion.16), channel_id=1, source_target_pairs={{0,6},{2,8},{4,10},{6,12},{8,14},{10,16},{12,18},{14,20},{16,22},{... | collective-permute-start | bytes 1572872 | tf_op jit(solution)/shard_map/ppermute | solution.py:17
  120.8 33.1 %collective-permute-start.7 = (bf16[4,128,512]{2,1,0:T(8,128)(2,1)S(1)}, bf16[4,128,512]{2,1,0:T(8,128)(2,1)}, u32[]{:S(2)}, u32[]{:S(2)}) collective-permute-start(bf16[4,128,512]{2,1,0:T(8,128)(2,1)S(1)} %pad_maximum_fusion.16), channel_id=1, source_target_pairs={{0,4},{2,6},{4,8},{6,10},{8,12},{10,14},{12,16},{14,18},{16,20},{1... | collective-permute-start | bytes 1572872 | tf_op jit(solution)/shard_map/ppermute | solution.py:17
  151.7 67.5 %collective-permute-start.27 = (bf16[3,16,64,640]{3,2,0,1:T(8,128)(2,1)}, bf16[3,16,64,640]{3,2,0,1:T(8,128)(2,1)S(1)}, u32[]{:S(2)}, u32[]{:S(2)}) collective-permute-start(bf16[3,16,64,640]{3,2,0,1:T(8,128)(2,1)} %get-tuple-element.94), channel_id=1, source_target_pairs={{0,2},{1,3},{2,0},{3,1},{4,6},{5,7},{6,4},{7,5},{8,10},{9,11},{10,... | collective-permute-start | bytes 11796488 | tf_op jit(solution)/shard_map/ppermute | solution.py:82
  187.2 35.5 %collective-permute-start.19 = (bf16[4,128,512]{2,1,0:T(8,128)(2,1)S(1)}, bf16[4,128,512]{2,1,0:T(8,128)(2,1)S(1)}, u32[]{:S(2)}, u32[]{:S(2)}) collective-permute-start(bf16[4,128,512]{2,1,0:T(8,128)(2,1)S(1)} %pad_maximum_fusion.17), channel_id=1, source_target_pairs={{0,8},{2,10},{4,12},{6,14},{8,16},{10,18},{12,20},{14,22},{16,24},... | collective-permute-start | bytes 1572872 | tf_op jit(solution)/shard_map/ppermute | solution.py:17
  290.6 34.3 %collective-permute-start.29 = (bf16[4,128,512]{2,1,0:T(8,128)(2,1)}, bf16[4,128,512]{2,1,0:T(8,128)(2,1)}, u32[]{:S(2)}, u32[]{:S(2)}) collective-permute-start(bf16[4,128,512]{2,1,0:T(8,128)(2,1)} %get-tuple-element.87), channel_id=1, source_target_pairs={{6,0},{8,2},{10,4},{12,6},{14,8},{16,10},{18,12},{20,14},{22,16},{... | collective-permute-start | bytes 1572872 | tf_op jit(solution)/shard_map/ppermute | solution.py:17
  291.9 33.1 %collective-permute-start.30 = (bf16[4,128,512]{2,1,0:T(8,128)(2,1)}, bf16[4,128,512]{2,1,0:T(8,128)(2,1)}, u32[]{:S(2)}, u32[]{:S(2)}) collective-permute-start(bf16[4,128,512]{2,1,0:T(8,128)(2,1)} %get-tuple-element.86), channel_id=1, source_target_pairs={{4,0},{6,2},{8,4},{10,6},{12,8},{14,10},{16,12},{18,14},{20,16},{2... | collective-permute-start | bytes 1572872 | tf_op jit(solution)/shard_map/ppermute | solution.py:17
  379.4 61.9 %collective-permute-start.32 = (bf16[4,128,512]{2,1,0:T(8,128)(2,1)}, bf16[4,128,512]{2,1,0:T(8,128)(2,1)}, u32[]{:S(2)}, u32[]{:S(2)}) collective-permute-start(bf16[4,128,512]{2,1,0:T(8,128)(2,1)} %get-tuple-element.78), channel_id=1, source_target_pairs={{8,0},{10,2},{12,4},{14,6},{16,8},{18,10},{20,12},{22,14},{24,16},... | collective-permute-start | bytes 1572872 | tf_op jit(solution)/shard_map/ppermute | solution.py:17
  380.8 60.5 %collective-permute-start.33 = (bf16[4,128,512]{2,1,0:T(8,128)(2,1)}, bf16[4,128,512]{2,1,0:T(8,128)(2,1)}, u32[]{:S(2)}, u32[]{:S(2)}) collective-permute-start(bf16[4,128,512]{2,1,0:T(8,128)(2,1)} %get-tuple-element.81), channel_id=1, source_target_pairs={{6,0},{8,2},{10,4},{12,6},{14,8},{16,10},{18,12},{20,14},{22,16},{... | collective-permute-start | bytes 1572872 | tf_op jit(solution)/shard_map/ppermute | solution.py:17
  382.1 60.4 %collective-permute-start.34 = (bf16[4,128,512]{2,1,0:T(8,128)(2,1)}, bf16[4,128,512]{2,1,0:T(8,128)(2,1)}, u32[]{:S(2)}, u32[]{:S(2)}) collective-permute-start(bf16[4,128,512]{2,1,0:T(8,128)(2,1)} %get-tuple-element.80), channel_id=1, source_target_pairs={{4,0},{6,2},{8,4},{10,6},{12,8},{14,10},{16,12},{18,14},{20,16},{2... | collective-permute-start | bytes 1572872 | tf_op jit(solution)/shard_map/ppermute | solution.py:17
  383.4 59.0 %collective-permute-start.35 = (bf16[4,128,512]{2,1,0:T(8,128)(2,1)}, bf16[4,128,512]{2,1,0:T(8,128)(2,1)}, u32[]{:S(2)}, u32[]{:S(2)}) collective-permute-start(bf16[4,128,512]{2,1,0:T(8,128)(2,1)} %get-tuple-element.79), channel_id=1, source_target_pairs={{2,0},{4,2},{6,4},{8,6},{10,8},{12,10},{14,12},{16,14},{18,16},{20... | collective-permute-start | bytes 1572872 | tf_op jit(solution)/shard_map/ppermute | solution.py:17
  434.1 71.0 %collective-permute-start.51 = (bf16[3,16,64,640]{3,2,1,0:T(8,128)(2,1)}, bf16[3,16,64,640]{3,2,1,0:T(8,128)(2,1)}, u32[]{:S(2)}, u32[]{:S(2)}) collective-permute-start(bf16[3,16,64,640]{3,2,1,0:T(8,128)(2,1)} %split.211), channel_id=1, source_target_pairs={{0,2},{1,3},{2,0},{3,1},{4,6},{5,7},{6,4},{7,5},{8,10},{9,11},{10,... | collective-permute-start | bytes 11796488 | tf_op jit(solution)/shard_map/ppermute | solution.py:82
  462.5 49.2 %collective-permute-start.46 = (bf16[3,16,64,640]{3,2,1,0:T(8,128)(2,1)}, bf16[3,16,64,640]{3,2,1,0:T(8,128)(2,1)}, u32[]{:S(2)}, u32[]{:S(2)}) collective-permute-start(bf16[3,16,64,640]{3,2,1,0:T(8,128)(2,1)} %split.201), channel_id=1, source_target_pairs={{0,2},{1,3},{2,0},{3,1},{4,6},{5,7},{6,4},{7,5},{8,10},{9,11},{10,... | collective-permute-start | bytes 11796488 | tf_op jit(solution)/shard_map/ppermute | solution.py:82
  515.4 50.3 %collective-permute-start.47 = (bf16[3,8,64,640]{3,2,1,0:T(8,128)(2,1)S(1)}, bf16[3,8,64,640]{3,2,1,0:T(8,128)(2,1)S(1)}, u32[]{:S(2)}, u32[]{:S(2)}) collective-permute-start(bf16[3,8,64,640]{3,2,1,0:T(8,128)(2,1)S(1)} %split.203), channel_id=1, source_target_pairs={{0,4},{1,5},{2,3},{3,2},{4,0},{5,1},{6,7},{7,6},{8,12},{9,13},{10,... | collective-permute-start | bytes 5898248 | tf_op jit(solution)/shard_map/ppermute | solution.py:82
  523.9 42.7 %collective-permute-start.40 = (bf16[1,80,640]{2,1,0:T(8,128)(2,1)S(1)}, bf16[1,80,640]{2,1,0:T(8,128)(2,1)S(1)}, u32[]{:S(2)}, u32[]{:S(2)}) collective-permute-start(bf16[1,80,640]{2,1,0:T(8,128)(2,1)S(1)} %broadcast_select_fusion.24), channel_id=1, source_target_pairs={{0,16},{1,17},{2,6},{3,7},{4,20},{5,21},{6,2},{7,3},{8,24},{9,25},... | collective-permute-start | bytes 307208 | tf_op jit(solution)/shard_map/ppermute | solution.py:82
  535.1 32.2 %collective-permute-start.53 = (bf16[3,4,64,640]{3,2,1,0:T(8,128)(2,1)S(1)}, bf16[3,4,64,640]{3,2,1,0:T(8,128)(2,1)S(1)}, u32[]{:S(2)}, u32[]{:S(2)}) collective-permute-start(bf16[3,4,64,640]{3,2,1,0:T(8,128)(2,1)S(1)} %split.215), channel_id=1, source_target_pairs={{0,1},{1,0},{2,10},{3,11},{4,5},{5,4},{6,14},{7,15},{8,9},{9,8},{1... | collective-permute-start | bytes 2949128 | tf_op jit(solution)/shard_map/ppermute | solution.py:82
  (195 other events, 2613.5 us)

commit v2 on v1

--- a/solution.py
+++ b/solution.py
@@ -92,11 +92,40 @@
     return (device_index() & exchange_plan()[0]) != 0
 
 
+class Transfer:
+    def __init__(self, steps):
+        self.steps = steps
+        self.result = None
+        self.flying = next(steps)
+
+    def push(self, came):
+        try:
+            self.flying = self.steps.send(came)
+        except StopIteration as stop:
+            self.flying = None
+            self.result = stop.value
+
+    def finish(self):
+        while self.flying is not None:
+            self.push(self.flying)
+        return self.result
+
+
+def advance(values, transfers):
+    live = [transfer for transfer in transfers if transfer.flying is not None]
+    if not live:
+        return values
+    values, came = lax.optimization_barrier((values, [transfer.flying for transfer in live]))
+    for transfer, arrived in zip(live, came):
+        transfer.push(arrived)
+    return values
+
+
 def gather_blocks(block, ordered, axis):
     core_bit, orders, upper_bits, wsh_bits = exchange_plan()
     held = jnp.expand_dims(block, axis)
     for pair in zip(*orders):
-        came = flip(held, pair)
+        came = yield flip(held, pair)
         if ordered:
             swap = my_bit(pair)
             held = jnp.concatenate(
@@ -104,7 +133,7 @@
             )
         else:
             held = jnp.concatenate([held, came], axis=axis)
-    came = flip(held, (core_bit, core_bit))
+    came = yield flip(held, (core_bit, core_bit))
     if not ordered:
         return jnp.concatenate([held, came], axis=axis)
     upper = is_upper_core()
@@ -140,14 +169,16 @@
         sent = jnp.where(upper, parts[0], parts[1])
     else:
         kept, sent = jnp.split(blocks, 2, axis=axis)
-    total = add_terms(kept, flip(sent, (core_bit, core_bit)))
+    came = yield flip(sent, (core_bit, core_bit))
+    total = add_terms(kept, came)
     for pair in list(zip(*orders))[::-1]:
         total = total.astype(jnp.bfloat16)
         kept, sent = jnp.split(total, 2, axis=axis)
         if ordered:
             swap = my_bit(pair)
             kept, sent = (jnp.where(swap, sent, kept), jnp.where(swap, kept, sent))
-        total = add_terms(kept, flip(sent, pair))
+        came = yield flip(sent, pair)
+        total = add_terms(kept, came)
     return jnp.squeeze(total, axis)
 
 
@@ -158,45 +189,47 @@
     return value
 
 
-def layer_weights(weights, layer_idx):
-    rows = [member[layer_idx] for member in weights]
-    attn = gather_blocks(jnp.concatenate(rows[:4], axis=0), True, 0)
-    ffn = gather_blocks(jnp.stack(rows[4:]), False, 1)
+def attn_gather(rows):
+    return Transfer(gather_blocks(jnp.concatenate(rows, axis=0), True, 0))
+
+
+def attn_mats(whole, rows):
     mats = []
     start = 0
-    for member in rows[:4]:
-        mats.append(attn[:, start : start + member.shape[0]].reshape(-1, member.shape[1]))
+    for member in rows:
+        mats.append(whole[:, start : start + member.shape[0]].reshape(-1, member.shape[1]))
         start += member.shape[0]
-    for kind in range(3):
-        mats.append(ffn[kind].reshape(-1, ffn.shape[-1]))
-    return tuple(mats)
-
-
-def share_attn(grads):
+    return mats
+
+
+def ffn_gather(rows):
+    return Transfer(gather_blocks(jnp.stack(rows), False, 1))
+
+
+def ffn_mats(whole):
+    return [whole[kind].reshape(-1, whole.shape[-1]) for kind in range(whole.shape[0])]
+
+
+def device_blocks(grads):
     count = lax.axis_size("seq") * lax.axis_size("wsh")
-    shaped = [
-        member.astype(jnp.bfloat16).reshape(count, -1, member.shape[1]) for member in grads
-    ]
-    summed = scatter_blocks(jnp.concatenate(shaped, axis=1), True, 0)
+    return [member.astype(jnp.bfloat16).reshape(count, -1, member.shape[1]) for member in grads]
+
+
+def attn_scatter(grads):
+    return Transfer(scatter_blocks(jnp.concatenate(device_blocks(grads), axis=1), True, 0))
+
+
+def attn_shares(summed, rows):
     shares = []
     start = 0
-    for member in shaped:
-        shares.append(summed[start : start + member.shape[1]])
-        start += member.shape[1]
+    for member in rows:
+        shares.append(summed[start : start + member.shape[0]])
+        start += member.shape[0]
     return shares
 
 
-def share_ffn(grads):
-    count = lax.axis_size("seq") * lax.axis_size("wsh")
-    stacked = jnp.stack(
-        [member.astype(jnp.bfloat16).reshape(count, -1, member.shape[1]) for member in grads]
-    )
-    summed = scatter_blocks(stacked, False, 1)
-    return [summed[kind] for kind in range(3)]
-
-
-def share_grads(grads):
-    return tuple(share_attn(grads[:4]) + share_ffn(grads[4:]))
+def ffn_scatter(grads):
+    return Transfer(scatter_blocks(jnp.stack(device_blocks(grads)), False, 1))
 
 
 def earlier_keys(packed_tokens, hop_count):
@@ -220,8 +253,10 @@
     return jnp.where(allowed[:, None], attention_scores, MASKED)
 
 
-def forward_layer(stream, gathered, gains, head_gain, angles, allowed, hop_count):
-    q_mat, k_mat, v_mat, o_mat, gate_mat, up_mat, down_mat = gathered
+def forward_layer(
+    stream, attn_weights, ffn_weights, gains, head_gain, angles, allowed, hop_count, tick
+):
+    q_mat, k_mat, v_mat, o_mat = attn_weights
     head_width = head_gain.shape[-1]
     head_count = q_mat.shape[0] // head_width
     batch_rows, group_len = (stream.shape[0], stream.shape[1])
@@ -233,6 +268,7 @@
     )
     rotated_query = query_rot(q_lin, head_gain[0], angles, head_count).astype(jnp.bfloat16)
     k_rot = key_rot(k_lin, head_gain[1], angles).astype(jnp.bfloat16)
+    rotated_query, k_rot, v_val = tick("projected", (rotated_query, k_rot, v_val))
     packed_tokens = earlier_keys(jnp.concatenate([k_rot, v_val], axis=-1), hop_count)
     attention_scores = masked_scores(rotated_query, packed_tokens[..., :head_width], allowed)
     row_max = jnp.max(attention_scores, axis=-1, keepdims=True)
@@ -247,14 +283,18 @@
         preferred_element_type=jnp.float32,
     )
     mixed = mixed.reshape(batch_rows, group_len, head_count * head_width).astype(jnp.bfloat16)
+    mixed = tick("mixed", mixed)
     attn_out = jnp.einsum("bce,ed->bcd", mixed, o_mat, preferred_element_type=jnp.float32)
     after_attn = stream + norm_gain(attn_out, gains[1])
     hidden = norm_gain(after_attn, gains[2]).astype(jnp.bfloat16)
+    after_attn, hidden = tick("hidden", (after_attn, hidden))
+    gate_mat, up_mat, down_mat = ffn_weights()
     gate_pre = jnp.einsum("bcd,fd->bcf", hidden, gate_mat, preferred_element_type=jnp.float32)
     up_pre = jnp.einsum("bcd,fd->bcf", hidden, up_mat, preferred_element_type=jnp.float32)
     activated = gelu_product(gate_pre, up_pre).astype(jnp.bfloat16)
+    activated = tick("activated", activated)
     down_out = jnp.einsum("bcf,fd->bcd", activated, down_mat, preferred_element_type=jnp.float32)
-    layer_out = after_attn + norm_gain(down_out, gains[3])
+    layer_out = tick("layer_out", after_attn + norm_gain(down_out, gains[3]))
     saved = (
         stream,
         normed,
@@ -272,10 +312,12 @@
         activated,
         down_out,
     )
-    return (saved, layer_out)
-
-
-def backward_layer(upstream, saved, gathered, gains, head_gain, angles, allowed, hop_count):
+    return (saved, (q_mat, k_mat, v_mat, o_mat, gate_mat, up_mat, down_mat), layer_out)
+
+
+def backward_layer(
+    upstream, saved, gathered, gains, head_gain, angles, allowed, hop_count, tick, send_ffn, send_attn
+):
     (
         stream,
         normed,
@@ -306,11 +348,14 @@
     d_gate, d_up = pullback(d_act)
     d_gate = d_gate.astype(jnp.bfloat16)
     d_up = d_up.astype(jnp.bfloat16)
+    d_gate, d_up = tick("d_gate", (d_gate, d_up))
     dw_gate = jnp.einsum("bcf,bcd->fd", d_gate, hidden, preferred_element_type=jnp.float32)
     dw_up = jnp.einsum("bcf,bcd->fd", d_up, hidden, preferred_element_type=jnp.float32)
     d_hidden = jnp.einsum(
         "bcf,fd->bcd", d_gate, gate_mat, preferred_element_type=jnp.float32
     ) + jnp.einsum("bcf,fd->bcd", d_up, up_mat, preferred_element_type=jnp.float32)
+    d_hidden = tick("d_hidden", d_hidden)
+    send_ffn((dw_gate, dw_up, dw_down))
     unused, pullback = jax.vjp(norm_gain, after_attn, gains[2])
     d_after, g_pre_ff = pullback(d_hidden)
     d_after = upstream + d_after
@@ -321,6 +366,7 @@
     mixed_gradient = jnp.einsum(
         "bcd,ed->bce", d_attn, o_mat, preferred_element_type=jnp.float32
     ).astype(jnp.bfloat16)
+    mixed_gradient = tick("d_mixed", mixed_gradient)
     mixed_gradient = mixed_gradient.reshape(batch_rows, group_len, head_count, head_width)
     key_matrix_rows = packed_tokens[..., :head_width]
     value_matrix_rows = packed_tokens[..., head_width:]
@@ -349,9 +395,9 @@
         mixed_gradient,
         preferred_element_type=jnp.float32,
     )
-    d_packed = returned_grads(
-        jnp.concatenate([key_gradient_rows, d_values], axis=-1), hop_count, group_len
-    )
+    d_packed = jnp.concatenate([key_gradient_rows, d_values], axis=-1)
+    d_packed, rotated_query_gradient = tick("d_packed", (d_packed, rotated_query_gradient))
+    d_packed = returned_grads(d_packed, hop_count, group_len)
 
     def query_part(lin_rows, gain_row):
         return query_rot(lin_rows, gain_row, angles, head_count)
@@ -376,11 +422,10 @@
     )
     unused, pullback = jax.vjp(norm_gain, stream, gains[0])
     d_stream, g_pre_attn = pullback(d_normed)
-    d_stream = d_after + d_stream
-    grads = (dw_query, dw_key, dw_value, dw_output, dw_gate, dw_up, dw_down)
+    d_stream = tick("d_stream", d_after + d_stream)
+    send_attn((dw_query, dw_key, dw_value, dw_output))
     return (
         d_stream,
-        grads,
         jnp.stack([g_pre_attn, g_post_attn, g_pre_ff, g_post_ff]),
         jnp.stack([g_query, g_key]),
     )
@@ -418,28 +463,77 @@
     )
     weights = (q_weight, k_weight, v_weight, o_weight, gate_weight, up_weight, down_weight)
     stream = tokens.astype(jnp.float32)
+    attn_rows = [[member[layer_idx] for member in weights[:4]] for layer_idx in range(layer_count)]
+    ffn_rows = [[member[layer_idx] for member in weights[4:]] for layer_idx in range(layer_count)]
+    attn_moves = [None] * layer_count
+    ffn_moves = [None] * layer_count
+    attn_moves[0] = attn_gather(attn_rows[0])
+    ffn_moves[0] = ffn_gather(ffn_rows[0])
+    attn_moves[0].finish()
+    for early in range(3):
+        ffn_moves[0].push(ffn_moves[0].flying)
     records = []
     for layer_idx in range(layer_count):
-        gathered = layer_weights(weights, layer_idx)
-        saved, stream = forward_layer(
+        following = layer_idx + 1 if layer_idx + 1 < layer_count else None
+
+        def tick(stage, values, layer_idx=layer_idx, following=following):
+            moves = []
+            if stage in ("projected", "mixed", "hidden"):
+                moves.append(ffn_moves[layer_idx])
+            if following is not None:
+                if stage == "projected":
+                    values, fresh = lax.optimization_barrier((values, attn_rows[following]))
+                    attn_moves[following] = attn_gather(fresh)
+                elif stage == "mixed":
+                    attn_moves[following].push(attn_moves[following].flying)
+                    moves.append(attn_moves[following])
+                elif stage == "hidden":
+                    moves.append(attn_moves[following])
+                    values, fresh = lax.optimization_barrier((values, ffn_rows[following]))
+                    ffn_moves[following] = ffn_gather(fresh)
+                else:
+                    moves.append(attn_moves[following])
+                    moves.append(ffn_moves[following])
+            return advance(values, moves)
+
+        def ffn_weights(layer_idx=layer_idx):
+            return ffn_mats(ffn_moves[layer_idx].finish())
+
+        saved, gathered, stream = forward_layer(
             stream,
-            gathered,
+            attn_mats(attn_moves[layer_idx].finish(), attn_rows[layer_idx]),
+            ffn_weights,
             norm_gains[layer_idx],
             head_gains[layer_idx],
             angles,
             allowed,
             hop_count,
+            tick,
         )
         records.append((saved, gathered))
     block_out = stream.astype(jnp.bfloat16)
     upstream = out_grad.astype(jnp.float32)
-    weight_shares = [None] * layer_count
     norm_parts = [None] * layer_count
     head_parts = [None] * layer_count
+    attn_sums = [None] * layer_count
+    ffn_sums = [None] * layer_count
+    sums = []
+
+    def back_tick(stage, values):
+        return advance(values, sums)
+
     for layer_idx in range(layer_count - 1, -1, -1):
-        saved, kept_mats = records[layer_idx]
-        gathered = kept_mats
-        upstream, grads, norm_part, head_part = backward_layer(
+        saved, gathered = records[layer_idx]
+
+        def send_ffn(grads, layer_idx=layer_idx):
+            ffn_sums[layer_idx] = ffn_scatter(grads)
+            sums.append(ffn_sums[layer_idx])
+
+        def send_attn(grads, layer_idx=layer_idx):
+            attn_sums[layer_idx] = attn_scatter(grads)
+            sums.append(attn_sums[layer_idx])
+
+        upstream, norm_parts[layer_idx], head_parts[layer_idx] = backward_layer(
             upstream,
             saved,
             gathered,
@@ -448,20 +542,21 @@
             angles,
             allowed,
             hop_count,
+            back_tick,
+            send_ffn,
+            send_attn,
         )
-        weight_shares[layer_idx] = share_grads(grads)
-        norm_parts[layer_idx] = norm_part
-        head_parts[layer_idx] = head_part
-    totals = [None] * layer_count
-    for layer_idx in range(layer_count - 1, -1, -1):
-        flat = jnp.concatenate(
-            [norm_parts[layer_idx].reshape(-1), head_parts[layer_idx].reshape(-1)]
+    weight_shares = []
+    for layer_idx in range(layer_count):
+        ffn_total = ffn_sums[layer_idx].finish()
+        weight_shares.append(
+            attn_shares(attn_sums[layer_idx].finish(), attn_rows[layer_idx])
+            + [ffn_total[kind] for kind in range(3)]
         )
-        totals[layer_idx] = sum_all(flat.reshape(-1, 128))
-    both = jnp.stack(totals).reshape(layer_count, -1)
-    norm_size = norm_gains[0].size
-    norm_total = both[:, :norm_size].reshape(norm_gains.shape)
-    head_total = both[:, norm_size:].reshape(head_gains.shape)
+    flat = jnp.concatenate([jnp.stack(norm_parts).reshape(-1), jnp.stack(head_parts).reshape(-1)])
+    both = sum_all(flat.reshape(-1, 128)).reshape(-1)
+    norm_total = both[: norm_gains.size].reshape(norm_gains.shape)
+    head_total = both[norm_gains.size :].reshape(head_gains.shape)
     stacked = tuple(
         (
             jnp.stack([weight_shares[layer_idx][member] for layer_idx in range(layer_count)])

time: 632 us -> 614 us (0.972)
  the two profiles are of different devices: /device:TPU:1 before, /device:TPU:0 now
where the time goes in v2:
time: 614 us; the launch traced here: 606 us
  waiting for transfers between devices  216 us (35%)
  starting transfers between devices  177 us (29%)
  matrix products  95.9 us (16%)
  other arithmetic  65.6 us (11%)
  local copies, waits for them, and re-layouts  46.8 us (8%)
    ppermute x45, waiting for transfers between devices, flip(): return lax.ppermute(value, ('seq', 'wsh'), pairs)  173 us
    ppermute x45, starting transfers between devices, flip(): return lax.ppermute(value, ('seq', 'wsh'), pairs)  145 us
    ppermute x16, waiting for transfers between devices, shifted(): lax.ppermute(value, axis, [(source, source + steps) for source in range(i...  42.2 us
    ppermute x16, starting transfers between devices, shifted(): lax.ppermute(value, axis, [(source, source + steps) for source in range(i...  31.8 us
    unnamed x293, local copies, waits for them, and re-layouts  18.6 us
    convert_element_type x16, other arithmetic, scatter_blocks(): total = total.astype(jnp.bfloat16)  13.9 us
  transfers between devices with their start and end apart: 61, of which 33 were waited for; matrix products, arithmetic and copies ran while one was open for 23% of the time, Pallas kernels for 0%

profile of v2, /device:TPU:0, one launch (start us, length us, event | category | flops | bytes accessed | tf_op | source)
XLA Modules:
  0.0 605.6 jit_solution(14197092918411009849)
XLA Ops:
  18.1 6.1 %collective-permute-done.2 = bf16[4,80,640]{2,1,0:T(8,128)(2,1)S(1)} collective-permute-done((bf16[4,80,640]{2,1,0:T(8,128)(2,1)S(1)}, bf16[4,80,640]{2,1,0:T(8,128)(2,1)S(1)}, u32[]{:S(2)}, u32[]{:S(2)}) %collective-permute-start.2) | collective-permute-done | bytes 409632 | tf_op jit(solution)/shard_map/ppermute | solution.py:82
  30.1 13.0 %collective-permute-done.5 = bf16[3,1,64,640]{3,2,0,1:T(8,128)(2,1)S(1)} collective-permute-done((bf16[3,1,64,640]{3,2,0,1:T(8,128)(2,1)S(1)}, bf16[3,1,64,640]{3,2,0,1:T(8,128)(2,1)S(1)}, u32[]{:S(2)}, u32[]{:S(2)}) %collective-permute-start.5) | collective-permute-done | bytes 245792 | tf_op jit(solution)/shard_map/ppermute | solution.py:82
  47.2 8.0 %collective-permute-done.6 = bf16[3,2,64,640]{3,2,0,1:T(8,128)(2,1)S(1)} collective-permute-done((bf16[3,2,64,640]{3,2,0,1:T(8,128)(2,1)S(1)}, bf16[3,2,64,640]{3,2,0,1:T(8,128)(2,1)S(1)}, u32[]{:S(2)}, u32[]{:S(2)}) %collective-permute-start.6) | collective-permute-done | bytes 491552 | tf_op jit(solution)/shard_map/ppermute | solution.py:82
  57.9 14.7 %collective-permute-done.7 = bf16[3,4,64,640]{3,2,0,1:T(8,128)(2,1)S(1)} collective-permute-done((bf16[3,4,64,640]{3,2,0,1:T(8,128)(2,1)S(1)}, bf16[3,4,64,640]{3,2,0,1:T(8,128)(2,1)S(1)}, u32[]{:S(2)}, u32[]{:S(2)}) %collective-permute-start.7) | collective-permute-done | bytes 983072 | tf_op jit(solution)/shard_map/ppermute | solution.py:82
  81.3 16.2 %collective-permute-done.8 = bf16[3,8,64,640]{3,2,0,1:T(8,128)(2,1)S(1)} collective-permute-done((bf16[3,8,64,640]{3,2,0,1:T(8,128)(2,1)S(1)}, bf16[3,8,64,640]{3,2,0,1:T(8,128)(2,1)S(1)}, u32[]{:S(2)}, u32[]{:S(2)}) %collective-permute-start.8) | collective-permute-done | bytes 1966112 | tf_op jit(solution)/shard_map/ppermute | solution.py:82
  114.2 6.0 collective-permute-done.9
  122.8 7.8 %collective-permute-done.11 = bf16[4,128,512]{2,1,0:T(8,128)(2,1)S(1)} collective-permute-done((bf16[4,128,512]{2,1,0:T(8,128)(2,1)S(1)}, bf16[4,128,512]{2,1,0:T(8,128)(2,1)S(1)}, u32[]{:S(2)}, u32[]{:S(2)}) %collective-permute-start.11) | collective-permute-done | bytes 524320 | tf_op jit(solution)/shard_map/ppermute | solution.py:17
  137.6 18.3 %collective-permute-start.18 = (bf16[3,1,64,640]{3,2,0,1:T(8,128)(2,1)S(1)}, bf16[3,1,64,640]{3,2,0,1:T(8,128)(2,1)S(1)}, u32[]{:S(2)}, u32[]{:S(2)}) collective-permute-start(bf16[3,1,64,640]{3,2,0,1:T(8,128)(2,1)S(1)} %maximum_bitcast_fusion.1), channel_id=1, source_target_pairs={{0,16},{1,17},{2,6},{3,7},{4,20},{5,21},{6,2},{7,3},{8,24},{9,25},... | collective-permute-start | bytes 737288 | tf_op jit(solution)/shard_map/ppermute | solution.py:82
  170.3 6.6 %collective-permute-done.17 = bf16[8,80,640]{2,1,0:T(8,128)(2,1)S(1)} collective-permute-done((bf16[8,80,640]{2,1,0:T(8,128)(2,1)S(1)}, bf16[8,80,640]{2,1,0:T(8,128)(2,1)S(1)}, u32[]{:S(2)}, u32[]{:S(2)}) %collective-permute-start.17) | collective-permute-done | bytes 819232 | tf_op jit(solution)/shard_map/ppermute | solution.py:82
  177.5 9.0 %collective-permute-start.20 = (bf16[3,2,64,640]{3,2,0,1:T(8,128)(2,1)S(1)}, bf16[3,2,64,640]{3,2,0,1:T(8,128)(2,1)S(1)}, u32[]{:S(2)}, u32[]{:S(2)}) collective-permute-start(bf16[3,2,64,640]{3,2,0,1:T(8,128)(2,1)S(1)} %pad_maximum_fusion.17), channel_id=1, source_target_pairs={{0,8},{1,9},{2,18},{3,19},{4,12},{5,13},{6,22},{7,23},{8,0},{9,1},... | collective-permute-start | bytes 1474568 | tf_op jit(solution)/shard_map/ppermute | solution.py:82
  201.4 6.9 %collective-permute-done.21 = bf16[3,4,64,640]{3,2,0,1:T(8,128)(2,1)S(1)} collective-permute-done((bf16[3,4,64,640]{3,2,0,1:T(8,128)(2,1)S(1)}, bf16[3,4,64,640]{3,2,0,1:T(8,128)(2,1)S(1)}, u32[]{:S(2)}, u32[]{:S(2)}) %collective-permute-start.21) | collective-permute-done | bytes 983072 | tf_op jit(solution)/shard_map/ppermute | solution.py:82
  224.4 10.4 %collective-permute-done.24 = bf16[4,128,512]{2,1,0:T(8,128)(2,1)S(1)} collective-permute-done((bf16[4,128,512]{2,1,0:T(8,128)(2,1)S(1)}, bf16[4,128,512]{2,1,0:T(8,128)(2,1)S(1)}, u32[]{:S(2)}, u32[]{:S(2)}) %collective-permute-start.24) | collective-permute-done | bytes 524320 | tf_op jit(solution)/shard_map/ppermute | solution.py:17
  239.6 18.4 %collective-permute-done.26 = bf16[3,8,64,640]{3,2,0,1:T(8,128)(2,1)S(1)} collective-permute-done((bf16[3,8,64,640]{3,2,0,1:T(8,128)(2,1)S(1)}, bf16[3,8,64,640]{3,2,0,1:T(8,128)(2,1)S(1)}, u32[]{:S(2)}, u32[]{:S(2)}) %collective-permute-start.26) | collective-permute-done | bytes 1966112 | tf_op jit(solution)/shard_map/ppermute | solution.py:82
  279.0 6.4 %multiply_convert_fusion.1 = (bf16[4,128,2048]{2,1,0:T(8,128)(2,1)S(1)}, bf16[4,128,2048]{2,1,0:T(8,128)(2,1)S(1)}) fusion(f32[4,128,2048]{2,1,0:T(8,128)S(1)} %fusion.104, f32[4,128,2048]{2,1,0:T(8,128)} %get-tuple-element.319, bf16[4,128,640]{2,1,0:T(8,128)(2,1)S(1)} %get-tuple-element.225, bf16[2048,640,1]{1,0,2:T(8,128)(2,1)S(1)} %bitcast.532), kind=kOutput, calls=%fused_computation.49 | convolution fusion | flops 1367343104 | bytes 15859712 | tf_op jit(solution)/shard_map/bcd,fd->bcf/dot_general | solution.py:346
  325.0 7.2 %collective-permute-done.29 = bf16[3,8,64,640]{3,2,1,0:T(8,128)(2,1)} collective-permute-done((bf16[3,8,64,640]{3,2,1,0:T(8,128)(2,1)}, bf16[3,8,64,640]{3,2,1,0:T(8,128)(2,1)}, u32[]{:S(2)}, u32[]{:S(2)}) %collective-permute-start.29) | collective-permute-done | bytes 1966112 | tf_op jit(solution)/shard_map/ppermute | solution.py:82
  352.0 13.0 %collective-permute-done.30 = bf16[4,128,512]{2,1,0:T(8,128)(2,1)S(1)} collective-permute-done((bf16[4,128,512]{2,1,0:T(8,128)(2,1)S(1)}, bf16[4,128,512]{2,1,0:T(8,128)(2,1)S(1)}, u32[]{:S(2)}, u32[]{:S(2)}) %collective-permute-start.30) | collective-permute-done | bytes 524320 | tf_op jit(solution)/shard_map/ppermute | solution.py:17
  369.8 11.1 %collective-permute-start.36 = (bf16[16,80,640]{2,1,0:T(8,128)(2,1)S(1)}, bf16[16,80,640]{2,1,0:T(8,128)(2,1)S(1)}, u32[]{:S(2)}, u32[]{:S(2)}) collective-permute-start(bf16[16,80,640]{2,1,0:T(8,128)(2,1)S(1)} %bitcast.539), channel_id=1, source_target_pairs={{0,2},{1,3},{2,0},{3,1},{4,6},{5,7},{6,4},{7,5},{8,10},{9,11},{10,... | collective-permute-start | bytes 4915208 | tf_op jit(solution)/shard_map/ppermute | solution.py:82
  386.1 22.3 %collective-permute-start.35 = (bf16[3,2,64,640]{3,2,1,0:T(8,128)(2,1)S(1)}, bf16[3,2,64,640]{3,2,1,0:T(8,128)(2,1)S(1)}, u32[]{:S(2)}, u32[]{:S(2)}) collective-permute-start(bf16[3,2,64,640]{3,2,1,0:T(8,128)(2,1)S(1)} %split.186), channel_id=1, source_target_pairs={{0,8},{1,9},{2,18},{3,19},{4,12},{5,13},{6,22},{7,23},{8,0},{9,1},... | collective-permute-start | bytes 1474568 | tf_op jit(solution)/shard_map/ppermute | solution.py:82
  423.6 6.4 %collective-permute-start.38 = (bf16[8,80,640]{2,1,0:T(8,128)(2,1)S(1)}, bf16[8,80,640]{2,1,0:T(8,128)(2,1)S(1)}, u32[]{:S(2)}, u32[]{:S(2)}) collective-permute-start(bf16[8,80,640]{2,1,0:T(8,128)(2,1)S(1)} %broadcast_select_fusion.7), channel_id=1, source_target_pairs={{0,4},{1,5},{2,3},{3,2},{4,0},{5,1},{6,7},{7,6},{8,12},{9,13},{10,... | collective-permute-start | bytes 2457608 | tf_op jit(solution)/shard_map/ppermute | solution.py:82
  474.2 8.7 %collective-permute-done.42 = bf16[3,8,64,640]{3,2,1,0:T(8,128)(2,1)} collective-permute-done((bf16[3,8,64,640]{3,2,1,0:T(8,128)(2,1)}, bf16[3,8,64,640]{3,2,1,0:T(8,128)(2,1)}, u32[]{:S(2)}, u32[]{:S(2)}) %collective-permute-start.42) | collective-permute-done | bytes 1966112 | tf_op jit(solution)/shard_map/ppermute | solution.py:82
  513.2 9.3 %collective-permute-start.56 = (f32[48,128]{1,0:T(8,128)S(1)}, f32[48,128]{1,0:T(8,128)S(1)}, u32[]{:S(2)}, u32[]{:S(2)}) collective-permute-start(f32[48,128]{1,0:T(8,128)S(1)} %maximum_bitcast_fusion.4), channel_id=1, source_target_pairs={{0,2},{1,3},{2,0},{3,1},{4,6},{5,7},{6,4},{7,5},{8,10},{9,11},{10,... | collective-permute-start | bytes 73736 | tf_op jit(solution)/shard_map/ppermute | solution.py:82
  526.3 21.1 %collective-permute-start.57 = (f32[48,128]{1,0:T(8,128)S(1)}, f32[48,128]{1,0:T(8,128)S(1)}, u32[]{:S(2)}, u32[]{:S(2)}) collective-permute-start(f32[48,128]{1,0:T(8,128)S(1)} %fusion.84), channel_id=1, source_target_pairs={{0,4},{1,5},{2,6},{3,7},{4,0},{5,1},{6,2},{7,3},{8,12},{9,13},{10,... | collective-permute-start | bytes 73736 | tf_op jit(solution)/shard_map/ppermute | solution.py:82
  569.1 10.0 %collective-permute-done.54 = bf16[3,2,64,640]{3,2,1,0:T(8,128)(2,1)S(1)} collective-permute-done((bf16[3,2,64,640]{3,2,1,0:T(8,128)(2,1)S(1)}, bf16[3,2,64,640]{3,2,1,0:T(8,128)(2,1)S(1)}, u32[]{:S(2)}, u32[]{:S(2)}) %collective-permute-start.54) | collective-permute-done | bytes 491552 | tf_op jit(solution)/shard_map/ppermute | solution.py:82
  583.2 5.3 collective-permute-done.55
  (681 shorter events, 339.0 us)
Async XLA Ops:
  24.4 21.3 %collective-permute-start.3 = (bf16[8,80,640]{2,1,0:T(8,128)(2,1)S(1)}, bf16[8,80,640]{2,1,0:T(8,128)(2,1)S(1)}, u32[]{:S(2)}, u32[]{:S(2)}) collective-permute-start(bf16[8,80,640]{2,1,0:T(8,128)(2,1)S(1)} %pad_maximum_fusion.14), channel_id=1, source_target_pairs={{0,4},{1,5},{2,3},{3,2},{4,0},{5,1},{6,7},{7,6},{8,12},{9,13},{10,... | collective-permute-start | bytes 2457608 | tf_op jit(solution)/shard_map/ppermute | solution.py:82
  46.0 27.9 %collective-permute-start.4 = (bf16[16,80,640]{2,1,0:T(8,128)(2,1)S(1)}, bf16[16,80,640]{2,1,0:T(8,128)(2,1)S(1)}, u32[]{:S(2)}, u32[]{:S(2)}) collective-permute-start(bf16[16,80,640]{2,1,0:T(8,128)(2,1)S(1)} %pad_maximum_fusion.10), channel_id=1, source_target_pairs={{0,2},{1,3},{2,0},{3,1},{4,6},{5,7},{6,4},{7,5},{8,10},{9,11},{10,... | collective-permute-start | bytes 4915208 | tf_op jit(solution)/shard_map/ppermute | solution.py:82
  72.8 24.7 %collective-permute-start.8 = (bf16[3,8,64,640]{3,2,0,1:T(8,128)(2,1)S(1)}, bf16[3,8,64,640]{3,2,0,1:T(8,128)(2,1)S(1)}, u32[]{:S(2)}, u32[]{:S(2)}) collective-permute-start(bf16[3,8,64,640]{3,2,0,1:T(8,128)(2,1)S(1)} %pad_maximum_fusion.8), channel_id=1, source_target_pairs={{0,4},{1,5},{2,3},{3,2},{4,0},{5,1},{6,7},{7,6},{8,12},{9,13},{10,... | collective-permute-start | bytes 5898248 | tf_op jit(solution)/shard_map/ppermute | solution.py:82
  98.4 37.0 %collective-permute-start.13 = (bf16[3,16,64,640]{3,2,0,1:T(8,128)(2,1)S(1)}, bf16[3,16,64,640]{3,2,0,1:T(8,128)(2,1)S(1)}, u32[]{:S(2)}, u32[]{:S(2)}) collective-permute-start(bf16[3,16,64,640]{3,2,0,1:T(8,128)(2,1)S(1)} %get-tuple-element.216), channel_id=1, source_target_pairs={{0,2},{1,3},{2,0},{3,1},{4,6},{5,7},{6,4},{7,5},{8,10},{9,11},{10,... | collective-permute-start | bytes 11796488 | tf_op jit(solution)/shard_map/ppermute | solution.py:82
  109.5 21.2 %collective-permute-start.11 = (bf16[4,128,512]{2,1,0:T(8,128)(2,1)S(1)}, bf16[4,128,512]{2,1,0:T(8,128)(2,1)S(1)}, u32[]{:S(2)}, u32[]{:S(2)}) collective-permute-start(bf16[4,128,512]{2,1,0:T(8,128)(2,1)S(1)} %constant_dynamic-update-slice_fusion), channel_id=1, source_target_pairs={{0,4},{2,6},{4,8},{6,10},{8,12},{10,14},{12,16},{14,18},{16,20},{1... | collective-permute-start | bytes 1572872 | tf_op jit(solution)/shard_map/ppermute | solution.py:17
  111.5 19.1 %collective-permute-start.12 = (bf16[4,128,512]{2,1,0:T(8,128)(2,1)S(1)}, bf16[4,128,512]{2,1,0:T(8,128)(2,1)S(1)}, u32[]{:S(2)}, u32[]{:S(2)}) collective-permute-start(bf16[4,128,512]{2,1,0:T(8,128)(2,1)S(1)} %constant_dynamic-update-slice_fusion), channel_id=1, source_target_pairs={{0,2},{2,4},{4,6},{6,8},{8,10},{10,12},{12,14},{14,16},{16,18},{18... | collective-permute-start | bytes 1572872 | tf_op jit(solution)/shard_map/ppermute | solution.py:17
  137.6 32.7 %collective-permute-start.18 = (bf16[3,1,64,640]{3,2,0,1:T(8,128)(2,1)S(1)}, bf16[3,1,64,640]{3,2,0,1:T(8,128)(2,1)S(1)}, u32[]{:S(2)}, u32[]{:S(2)}) collective-permute-start(bf16[3,1,64,640]{3,2,0,1:T(8,128)(2,1)S(1)} %maximum_bitcast_fusion.1), channel_id=1, source_target_pairs={{0,16},{1,17},{2,6},{3,7},{4,20},{5,21},{6,2},{7,3},{8,24},{9,25},... | collective-permute-start | bytes 737288 | tf_op jit(solution)/shard_map/ppermute | solution.py:82
  213.6 21.2 %collective-permute-start.24 = (bf16[4,128,512]{2,1,0:T(8,128)(2,1)S(1)}, bf16[4,128,512]{2,1,0:T(8,128)(2,1)S(1)}, u32[]{:S(2)}, u32[]{:S(2)}) collective-permute-start(bf16[4,128,512]{2,1,0:T(8,128)(2,1)S(1)} %constant_dynamic-update-slice_fusion.19), channel_id=1, source_target_pairs={{0,4},{2,6},{4,8},{6,10},{8,12},{10,14},{12,16},{14,18},{16,20},{1... | collective-permute-start | bytes 1572872 | tf_op jit(solution)/shard_map/ppermute | solution.py:17
  219.2 38.8 %collective-permute-start.26 = (bf16[3,8,64,640]{3,2,0,1:T(8,128)(2,1)S(1)}, bf16[3,8,64,640]{3,2,0,1:T(8,128)(2,1)S(1)}, u32[]{:S(2)}, u32[]{:S(2)}) collective-permute-start(bf16[3,8,64,640]{3,2,0,1:T(8,128)(2,1)S(1)} %pad_maximum_fusion.9), channel_id=1, source_target_pairs={{0,4},{1,5},{2,3},{3,2},{4,0},{5,1},{6,7},{7,6},{8,12},{9,13},{10,... | collective-permute-start | bytes 5898248 | tf_op jit(solution)/shard_map/ppermute | solution.py:82
  306.8 25.4 %collective-permute-start.29 = (bf16[3,8,64,640]{3,2,1,0:T(8,128)(2,1)}, bf16[3,8,64,640]{3,2,1,0:T(8,128)(2,1)}, u32[]{:S(2)}, u32[]{:S(2)}) collective-permute-start(bf16[3,8,64,640]{3,2,1,0:T(8,128)(2,1)} %split.178), channel_id=1, source_target_pairs={{0,4},{1,5},{2,3},{3,2},{4,0},{5,1},{6,7},{7,6},{8,12},{9,13},{10,... | collective-permute-start | bytes 5898248 | tf_op jit(solution)/shard_map/ppermute | solution.py:82
  340.1 24.9 %collective-permute-start.30 = (bf16[4,128,512]{2,1,0:T(8,128)(2,1)S(1)}, bf16[4,128,512]{2,1,0:T(8,128)(2,1)S(1)}, u32[]{:S(2)}, u32[]{:S(2)}) collective-permute-start(bf16[4,128,512]{2,1,0:T(8,128)(2,1)S(1)} %get-tuple-element.203), channel_id=1, source_target_pairs={{8,0},{10,2},{12,4},{14,6},{16,8},{18,10},{20,12},{22,14},{24,16},... | collective-permute-start | bytes 1572872 | tf_op jit(solution)/shard_map/ppermute | solution.py:17
  341.7 23.3 %collective-permute-start.31 = (bf16[4,128,512]{2,1,0:T(8,128)(2,1)S(1)}, bf16[4,128,512]{2,1,0:T(8,128)(2,1)S(1)}, u32[]{:S(2)}, u32[]{:S(2)}) collective-permute-start(bf16[4,128,512]{2,1,0:T(8,128)(2,1)S(1)} %get-tuple-element.206), channel_id=1, source_target_pairs={{6,0},{8,2},{10,4},{12,6},{14,8},{16,10},{18,12},{20,14},{22,16},{... | collective-permute-start | bytes 1572872 | tf_op jit(solution)/shard_map/ppermute | solution.py:17
  343.0 22.0 %collective-permute-start.32 = (bf16[4,128,512]{2,1,0:T(8,128)(2,1)S(1)}, bf16[4,128,512]{2,1,0:T(8,128)(2,1)S(1)}, u32[]{:S(2)}, u32[]{:S(2)}) collective-permute-start(bf16[4,128,512]{2,1,0:T(8,128)(2,1)S(1)} %get-tuple-element.205), channel_id=1, source_target_pairs={{4,0},{6,2},{8,4},{10,6},{12,8},{14,10},{16,12},{18,14},{20,16},{2... | collective-permute-start | bytes 1572872 | tf_op jit(solution)/shard_map/ppermute | solution.py:17
  344.3 20.7 %collective-permute-start.33 = (bf16[4,128,512]{2,1,0:T(8,128)(2,1)S(1)}, bf16[4,128,512]{2,1,0:T(8,128)(2,1)S(1)}, u32[]{:S(2)}, u32[]{:S(2)}) collective-permute-start(bf16[4,128,512]{2,1,0:T(8,128)(2,1)S(1)} %get-tuple-element.204), channel_id=1, source_target_pairs={{2,0},{4,2},{6,4},{8,6},{10,8},{12,10},{14,12},{16,14},{18,16},{20... | collective-permute-start | bytes 1572872 | tf_op jit(solution)/shard_map/ppermute | solution.py:17
  348.0 37.7 %collective-permute-start.34 = (bf16[3,4,64,640]{3,2,1,0:T(8,128)(2,1)S(1)}, bf16[3,4,64,640]{3,2,1,0:T(8,128)(2,1)S(1)}, u32[]{:S(2)}, u32[]{:S(2)}) collective-permute-start(bf16[3,4,64,640]{3,2,1,0:T(8,128)(2,1)S(1)} %split.184), channel_id=1, source_target_pairs={{0,1},{1,0},{2,10},{3,11},{4,5},{5,4},{6,14},{7,15},{8,9},{9,8},{1... | collective-permute-start | bytes 2949128 | tf_op jit(solution)/shard_map/ppermute | solution.py:82
  369.8 47.9 %collective-permute-start.36 = (bf16[16,80,640]{2,1,0:T(8,128)(2,1)S(1)}, bf16[16,80,640]{2,1,0:T(8,128)(2,1)S(1)}, u32[]{:S(2)}, u32[]{:S(2)}) collective-permute-start(bf16[16,80,640]{2,1,0:T(8,128)(2,1)S(1)} %bitcast.539), channel_id=1, source_target_pairs={{0,2},{1,3},{2,0},{3,1},{4,6},{5,7},{6,4},{7,5},{8,10},{9,11},{10,... | collective-permute-start | bytes 4915208 | tf_op jit(solution)/shard_map/ppermute | solution.py:82
  386.1 31.6 %collective-permute-start.35 = (bf16[3,2,64,640]{3,2,1,0:T(8,128)(2,1)S(1)}, bf16[3,2,64,640]{3,2,1,0:T(8,128)(2,1)S(1)}, u32[]{:S(2)}, u32[]{:S(2)}) collective-permute-start(bf16[3,2,64,640]{3,2,1,0:T(8,128)(2,1)S(1)} %split.186), channel_id=1, source_target_pairs={{0,8},{1,9},{2,18},{3,19},{4,12},{5,13},{6,22},{7,23},{8,0},{9,1},... | collective-permute-start | bytes 1474568 | tf_op jit(solution)/shard_map/ppermute | solution.py:82
  423.1 31.8 %collective-permute-start.40 = (bf16[3,16,64,640]{3,2,1,0:T(8,128)(2,1)S(1)}, bf16[3,16,64,640]{3,2,1,0:T(8,128)(2,1)S(1)}, u32[]{:S(2)}, u32[]{:S(2)}) collective-permute-start(bf16[3,16,64,640]{3,2,1,0:T(8,128)(2,1)S(1)} %split.193), channel_id=1, source_target_pairs={{0,2},{1,3},{2,0},{3,1},{4,6},{5,7},{6,4},{7,5},{8,10},{9,11},{10,... | collective-permute-start | bytes 11796488 | tf_op jit(solution)/shard_map/ppermute | solution.py:82
  423.6 19.4 %collective-permute-start.38 = (bf16[8,80,640]{2,1,0:T(8,128)(2,1)S(1)}, bf16[8,80,640]{2,1,0:T(8,128)(2,1)S(1)}, u32[]{:S(2)}, u32[]{:S(2)}) collective-permute-start(bf16[8,80,640]{2,1,0:T(8,128)(2,1)S(1)} %broadcast_select_fusion.7), channel_id=1, source_target_pairs={{0,4},{1,5},{2,3},{3,2},{4,0},{5,1},{6,7},{7,6},{8,12},{9,13},{10,... | collective-permute-start | bytes 2457608 | tf_op jit(solution)/shard_map/ppermute | solution.py:82
  457.9 24.9 %collective-permute-start.42 = (bf16[3,8,64,640]{3,2,1,0:T(8,128)(2,1)}, bf16[3,8,64,640]{3,2,1,0:T(8,128)(2,1)}, u32[]{:S(2)}, u32[]{:S(2)}) collective-permute-start(bf16[3,8,64,640]{3,2,1,0:T(8,128)(2,1)} %split.197), channel_id=1, source_target_pairs={{0,4},{1,5},{2,3},{3,2},{4,0},{5,1},{6,7},{7,6},{8,12},{9,13},{10,... | collective-permute-start | bytes 5898248 | tf_op jit(solution)/shard_map/ppermute | solution.py:82
  484.6 18.3 %collective-permute-start.43 = (bf16[4,128,512]{2,1,0:T(8,128)(2,1)}, bf16[4,128,512]{2,1,0:T(8,128)(2,1)}, u32[]{:S(2)}, u32[]{:S(2)}) collective-permute-start(bf16[4,128,512]{2,1,0:T(8,128)(2,1)} %get-tuple-element.197), channel_id=1, source_target_pairs={{8,0},{10,2},{12,4},{14,6},{16,8},{18,10},{20,12},{22,14},{24,16},... | collective-permute-start | bytes 1572872 | tf_op jit(solution)/shard_map/ppermute | solution.py:17
  499.0 64.3 %collective-permute-start.48 = (bf16[3,4,64,640]{3,2,1,0:T(8,128)(2,1)}, bf16[3,4,64,640]{3,2,1,0:T(8,128)(2,1)}, u32[]{:S(2)}, u32[]{:S(2)}) collective-permute-start(bf16[3,4,64,640]{3,2,1,0:T(8,128)(2,1)} %split.205), channel_id=1, source_target_pairs={{0,1},{1,0},{2,10},{3,11},{4,5},{5,4},{6,14},{7,15},{8,9},{9,8},{1... | collective-permute-start | bytes 2949128 | tf_op jit(solution)/shard_map/ppermute | solution.py:82
  526.3 39.4 %collective-permute-start.49 = (bf16[16,80,640]{2,1,0:T(8,128)(2,1)}, bf16[16,80,640]{2,1,0:T(8,128)(2,1)}, u32[]{:S(2)}, u32[]{:S(2)}) collective-permute-start(bf16[16,80,640]{2,1,0:T(8,128)(2,1)} %bitcast.155), channel_id=1, source_target_pairs={{0,2},{1,3},{2,0},{3,1},{4,6},{5,7},{6,4},{7,5},{8,10},{9,11},{10,... | collective-permute-start | bytes 4915208 | tf_op jit(solution)/shard_map/ppermute | solution.py:82
  526.3 23.0 %collective-permute-start.57 = (f32[48,128]{1,0:T(8,128)S(1)}, f32[48,128]{1,0:T(8,128)S(1)}, u32[]{:S(2)}, u32[]{:S(2)}) collective-permute-start(f32[48,128]{1,0:T(8,128)S(1)} %fusion.84), channel_id=1, source_target_pairs={{0,4},{1,5},{2,6},{3,7},{4,0},{5,1},{6,2},{7,3},{8,12},{9,13},{10,... | collective-permute-start | bytes 73736 | tf_op jit(solution)/shard_map/ppermute | solution.py:82
  (173 other events, 2360.6 us)

commit v3 on v2

--- a/solution.py
+++ b/solution.py
@@ -185,7 +185,8 @@
 def sum_all(value):
     core_bit, orders, upper_bits, wsh_bits = exchange_plan()
     for bit in [core_bit] + upper_bits[::-1] + wsh_bits:
-        value = value + flip(value, (bit, bit))
+        came = yield flip(value, (bit, bit))
+        value = value + came
     return value
 
 
@@ -232,18 +233,48 @@
     return Transfer(scatter_blocks(jnp.stack(device_blocks(grads)), False, 1))
 
 
-def earlier_keys(packed_tokens, hop_count):
-    pieces = [shifted(packed_tokens, "seq", hop) for hop in range(hop_count, 0, -1)]
-    return jnp.concatenate(pieces + [packed_tokens], axis=1)
+def exchange_rows(blocks):
+    count = blocks.shape[0]
+    total = lax.axis_size("seq")
+    place = lax.axis_index("seq") % count
+
+    def by_distance(value):
+        step = 1
+        while step < count:
+            swapped = jnp.stack([value[index ^ step] for index in range(count)])
+            value = jnp.where((place & step) != 0, swapped, value)
+            step *= 2
+        return value
+
+    outgoing = by_distance(blocks)
+    arrived = [outgoing[0]]
+    for step in range(1, count):
+        pairs = [(source, source ^ step) for source in range(total)]
+        arrived.append(lax.ppermute(outgoing[step], "seq", pairs))
+    return by_distance(jnp.stack(arrived))
+
+
+def context_blocks(packed_tokens, hop_count):
+    group_count, group_len, width = packed_tokens.shape
+    before = shifted(packed_tokens, "seq", group_count)
+    line = jnp.concatenate([before, packed_tokens], axis=0).reshape(-1, width)
+    span = (hop_count + 1) * group_len
+    return jnp.stack(
+        [line[group * group_len : group * group_len + span] for group in range(group_count)]
+    )
 
 
 def returned_grads(grad_all, hop_count, group_len):
-    summed = grad_all[:, hop_count * group_len :]
-    for hop in range(hop_count, 0, -1):
-        start = (hop_count - hop) * group_len
-        piece = grad_all[:, start : start + group_len].astype(jnp.bfloat16)
-        summed = summed + shifted(piece, "seq", -hop).astype(jnp.float32)
-    return summed
+    group_count = grad_all.shape[0]
+    slots = [None] * (2 * group_count)
+    for group in range(group_count):
+        for hop in range(hop_count + 1):
+            piece = grad_all[group, hop * group_len : (hop + 1) * group_len]
+            slot = group + hop
+            slots[slot] = piece if slots[slot] is None else slots[slot] + piece
+    outgoing = jnp.stack(slots[:group_count]).astype(jnp.bfloat16)
+    came = shifted(outgoing, "seq", -group_count)
+    return jnp.stack(slots[group_count:]) + came.astype(jnp.float32)
 
 
 def masked_scores(rotated_query, key_matrix_rows, allowed):
@@ -269,7 +300,7 @@
     rotated_query = query_rot(q_lin, head_gain[0], angles, head_count).astype(jnp.bfloat16)
     k_rot = key_rot(k_lin, head_gain[1], angles).astype(jnp.bfloat16)
     rotated_query, k_rot, v_val = tick("projected", (rotated_query, k_rot, v_val))
-    packed_tokens = earlier_keys(jnp.concatenate([k_rot, v_val], axis=-1), hop_count)
+    packed_tokens = context_blocks(jnp.concatenate([k_rot, v_val], axis=-1), hop_count)
     attention_scores = masked_scores(rotated_query, packed_tokens[..., :head_width], allowed)
     row_max = jnp.max(attention_scores, axis=-1, keepdims=True)
     log_total = row_max + jnp.log(
@@ -449,6 +480,11 @@
     layer_count = q_weight.shape[0]
     head_width = head_gains.shape[-1]
     hop_count = WINDOW // group_len
+    marks = (group_offset // group_len).astype(tokens.dtype)
+    marks = jnp.broadcast_to(marks[:, :, None], (tokens.shape[0], 16, tokens.shape[2]))
+    tokens = exchange_rows(jnp.concatenate([tokens, marks], axis=1))
+    group_offset = tokens[:, group_len, :1].astype(jnp.int32) * group_len
+    tokens = tokens[:, :group_len]
     position = group_offset + jnp.arange(group_len, dtype=jnp.int32)[None, :]
     angles = position.astype(jnp.float32)[..., None] * frequencies(head_width)[None, None, :]
     angles = lax.optimization_barrier((jnp.cos(angles), jnp.sin(angles)))
@@ -511,7 +547,8 @@
             tick,
         )
         records.append((saved, gathered))
-    block_out = stream.astype(jnp.bfloat16)
+    block_out = exchange_rows(stream.astype(jnp.bfloat16))
+    out_grad = exchange_rows(out_grad)
     upstream = out_grad.astype(jnp.float32)
     norm_parts = [None] * layer_count
     head_parts = [None] * layer_count
@@ -546,15 +583,20 @@
             send_ffn,
             send_attn,
         )
+    flat = jnp.concatenate([jnp.stack(norm_parts).reshape(-1), jnp.stack(head_parts).reshape(-1)])
+    gains_sum = Transfer(sum_all(flat.reshape(-1, 128)))
+    sums.append(gains_sum)
+    while any(move.flying is not None for move in sums):
+        advance((), sums)
+    upstream = exchange_rows(upstream.astype(jnp.bfloat16)).astype(jnp.float32)
     weight_shares = []
     for layer_idx in range(layer_count):
-        ffn_total = ffn_sums[layer_idx].finish()
+        ffn_total = ffn_sums[layer_idx].result
         weight_shares.append(
-            attn_shares(attn_sums[layer_idx].finish(), attn_rows[layer_idx])
+            attn_shares(attn_sums[layer_idx].result, attn_rows[layer_idx])
             + [ffn_total[kind] for kind in range(3)]
         )
-    flat = jnp.concatenate([jnp.stack(norm_parts).reshape(-1), jnp.stack(head_parts).reshape(-1)])
-    both = sum_all(flat.reshape(-1, 128)).reshape(-1)
+    both = gains_sum.result.reshape(-1)
     norm_total = both[: norm_gains.size].reshape(norm_gains.shape)
     head_total = both[norm_gains.size :].reshape(head_gains.shape)
     stacked = tuple(

time: 614 us -> 508 us (0.83)
  starting transfers between devices: 177 us -> 87.3 us
  waiting for transfers between devices: 216 us -> 183 us
  other arithmetic: 65.6 us -> 73.9 us
    ppermute x45, starting transfers between devices: 145 us -> 69.2 us  [flip(): return lax.ppermute(value, ('seq', 'wsh'), pairs)]
    ppermute x45, waiting for transfers between devices: 173 us -> 142 us  [flip(): return lax.ppermute(value, ('seq', 'wsh'), pairs)]
    ppermute x16 -> x4, starting transfers between devices: 31.8 us -> 7.89 us  [shifted(): lax.ppermute(value, axis, [(source, source + steps) for source in range(i...]
    ppermute x16 -> x4, waiting for transfers between devices: 42.2 us -> 23.6 us  [shifted(): lax.ppermute(value, axis, [(source, source + steps) for source in range(i...]
    ppermute x0 -> x12, waiting for transfers between devices: none -> 17.1 us  [exchange_rows(): arrived.append(lax.ppermute(outgoing[step], 'seq', pairs))]
    ppermute x0 -> x12, starting transfers between devices: none -> 10.2 us  [exchange_rows(): arrived.append(lax.ppermute(outgoing[step], 'seq', pairs))]
    unnamed x293 -> x355, local copies, waits for them, and re-layouts: 18.6 us -> 25.1 us
  transfers between devices with their start and end apart: 61 -> 61, of which waited for: 33 -> 33; matrix products, arithmetic and copies ran while one was open for 23% -> 28% of each run, Pallas kernels for 0% -> 0%
where the time goes in v3:
time: 508 us; the launch traced here: 500 us
  waiting for transfers between devices  183 us (36%)
  matrix products  99.1 us (20%)
  starting transfers between devices  87.3 us (17%)
  other arithmetic  73.9 us (15%)
  local copies, waits for them, and re-layouts  51.8 us (10%)
    ppermute x45, waiting for transfers between devices, flip(): return lax.ppermute(value, ('seq', 'wsh'), pairs)  142 us
    ppermute x45, starting transfers between devices, flip(): return lax.ppermute(value, ('seq', 'wsh'), pairs)  69.2 us
    unnamed x355, local copies, waits for them, and re-layouts  25.1 us
    ppermute x4, waiting for transfers between devices, shifted(): lax.ppermute(value, axis, [(source, source + steps) for source in range(i...  23.6 us
    ppermute x12, waiting for transfers between devices, exchange_rows(): arrived.append(lax.ppermute(outgoing[step], 'seq', pairs))  17.1 us
    dot_general x2, matrix products, backward_layer(): jnp.einsum('bcd,fd->bcf', d_down, down_mat, preferred_element_type=jnp.fl...  12.4 us
    convert_element_type x16, other arithmetic, scatter_blocks(): total = total.astype(jnp.bfloat16)  12.3 us
    ppermute x12, starting transfers between devices, exchange_rows(): arrived.append(lax.ppermute(outgoing[step], 'seq', pairs))  10.2 us
  transfers between devices with their start and end apart: 61, of which 33 were waited for; matrix products, arithmetic and copies ran while one was open for 28% of the time, Pallas kernels for 0%

profile of v3, /device:TPU:0, one launch (start us, length us, event | category | flops | bytes accessed | tf_op | source)
XLA Modules:
  0.0 499.6 jit_solution(14489837933964576102)
XLA Ops:
  22.3 5.4 %collective-permute-done.5 = bf16[4,80,640]{2,1,0:T(8,128)(2,1)S(1)} collective-permute-done((bf16[4,80,640]{2,1,0:T(8,128)(2,1)S(1)}, bf16[4,80,640]{2,1,0:T(8,128)(2,1)S(1)}, u32[]{:S(2)}, u32[]{:S(2)}) %collective-permute-start.5) | collective-permute-done | bytes 409632 | tf_op jit(solution)/shard_map/ppermute | solution.py:82
  32.2 8.1 %collective-permute-done.6 = bf16[8,80,640]{2,1,0:T(8,128)(2,1)S(1)} collective-permute-done((bf16[8,80,640]{2,1,0:T(8,128)(2,1)S(1)}, bf16[8,80,640]{2,1,0:T(8,128)(2,1)S(1)}, u32[]{:S(2)}, u32[]{:S(2)}) %collective-permute-start.6) | collective-permute-done | bytes 819232 | tf_op jit(solution)/shard_map/ppermute | solution.py:82
  40.6 12.4 %collective-permute-start.7 = (bf16[16,80,640]{2,1,0:T(8,128)(2,1)S(1)}, bf16[16,80,640]{2,1,0:T(8,128)(2,1)S(1)}, u32[]{:S(2)}, u32[]{:S(2)}) collective-permute-start(bf16[16,80,640]{2,1,0:T(8,128)(2,1)S(1)} %pad_maximum_fusion.13), channel_id=1, source_target_pairs={{0,2},{1,3},{2,0},{3,1},{4,6},{5,7},{6,4},{7,5},{8,10},{9,11},{10,... | collective-permute-start | bytes 4915208 | tf_op jit(solution)/shard_map/ppermute | solution.py:82
  56.4 11.0 %collective-permute-done.10 = bf16[3,4,64,640]{3,2,0,1:T(8,128)(2,1)S(1)} collective-permute-done((bf16[3,4,64,640]{3,2,0,1:T(8,128)(2,1)S(1)}, bf16[3,4,64,640]{3,2,0,1:T(8,128)(2,1)S(1)}, u32[]{:S(2)}, u32[]{:S(2)}) %collective-permute-start.10) | collective-permute-done | bytes 983072 | tf_op jit(solution)/shard_map/ppermute | solution.py:82
  77.4 15.0 %collective-permute-done.11 = bf16[3,8,64,640]{3,2,0,1:T(8,128)(2,1)S(1)} collective-permute-done((bf16[3,8,64,640]{3,2,0,1:T(8,128)(2,1)S(1)}, bf16[3,8,64,640]{3,2,0,1:T(8,128)(2,1)S(1)}, u32[]{:S(2)}, u32[]{:S(2)}) %collective-permute-start.11) | collective-permute-done | bytes 1966112 | tf_op jit(solution)/shard_map/ppermute | solution.py:82
  100.9 8.4 %collective-permute-done.12 = bf16[4,128,512]{2,1,0:T(8,128)(2,1)S(1)} collective-permute-done((bf16[4,128,512]{2,1,0:T(8,128)(2,1)S(1)}, bf16[4,128,512]{2,1,0:T(8,128)(2,1)S(1)}, u32[]{:S(2)}, u32[]{:S(2)}) %collective-permute-start.12) | collective-permute-done | bytes 524320 | tf_op jit(solution)/shard_map/ppermute | solution.py:17
  116.8 5.8 %collective-permute-start.18 = (bf16[3,1,64,640]{3,2,0,1:T(8,128)(2,1)S(1)}, bf16[3,1,64,640]{3,2,0,1:T(8,128)(2,1)S(1)}, u32[]{:S(2)}, u32[]{:S(2)}) collective-permute-start(bf16[3,1,64,640]{3,2,0,1:T(8,128)(2,1)S(1)} %maximum_bitcast_fusion.1), channel_id=1, source_target_pairs={{0,16},{1,17},{2,6},{3,7},{4,20},{5,21},{6,2},{7,3},{8,24},{9,25},... | collective-permute-start | bytes 737288 | tf_op jit(solution)/shard_map/ppermute | solution.py:82
  124.9 6.8 %collective-permute-done.16 = bf16[4,80,640]{2,1,0:T(8,128)(2,1)S(1)} collective-permute-done((bf16[4,80,640]{2,1,0:T(8,128)(2,1)S(1)}, bf16[4,80,640]{2,1,0:T(8,128)(2,1)S(1)}, u32[]{:S(2)}, u32[]{:S(2)}) %collective-permute-start.16) | collective-permute-done | bytes 409632 | tf_op jit(solution)/shard_map/ppermute | solution.py:82
  131.9 6.1 %collective-permute-start.17 = (bf16[8,80,640]{2,1,0:T(8,128)(2,1)S(1)}, bf16[8,80,640]{2,1,0:T(8,128)(2,1)S(1)}, u32[]{:S(2)}, u32[]{:S(2)}) collective-permute-start(bf16[8,80,640]{2,1,0:T(8,128)(2,1)S(1)} %pad_maximum_fusion.18), channel_id=1, source_target_pairs={{0,4},{1,5},{2,3},{3,2},{4,0},{5,1},{6,7},{7,6},{8,12},{9,13},{10,... | collective-permute-start | bytes 2457608 | tf_op jit(solution)/shard_map/ppermute | solution.py:82
  143.7 4.6 collective-permute-done.17
  151.3 11.7 %collective-permute-done.20 = bf16[3,2,64,640]{3,2,0,1:T(8,128)(2,1)S(1)} collective-permute-done((bf16[3,2,64,640]{3,2,0,1:T(8,128)(2,1)S(1)}, bf16[3,2,64,640]{3,2,0,1:T(8,128)(2,1)S(1)}, u32[]{:S(2)}, u32[]{:S(2)}) %collective-permute-start.20) | collective-permute-done | bytes 491552 | tf_op jit(solution)/shard_map/ppermute | solution.py:82
  169.9 7.4 %collective-permute-done.21 = bf16[3,4,64,640]{3,2,0,1:T(8,128)(2,1)S(1)} collective-permute-done((bf16[3,4,64,640]{3,2,0,1:T(8,128)(2,1)S(1)}, bf16[3,4,64,640]{3,2,0,1:T(8,128)(2,1)S(1)}, u32[]{:S(2)}, u32[]{:S(2)}) %collective-permute-start.21) | collective-permute-done | bytes 983072 | tf_op jit(solution)/shard_map/ppermute | solution.py:82
  182.4 4.9 collective-permute-done.22
  192.5 12.0 %collective-permute-done.23 = bf16[3,8,64,640]{3,2,0,1:T(8,128)(2,1)S(1)} collective-permute-done((bf16[3,8,64,640]{3,2,0,1:T(8,128)(2,1)S(1)}, bf16[3,8,64,640]{3,2,0,1:T(8,128)(2,1)S(1)}, u32[]{:S(2)}, u32[]{:S(2)}) %collective-permute-start.23) | collective-permute-done | bytes 1966112 | tf_op jit(solution)/shard_map/ppermute | solution.py:82
  231.9 7.8 %multiply_convert_fusion.1 = (bf16[4,128,2048]{2,1,0:T(8,128)(2,1)S(1)}, bf16[4,128,2048]{2,1,0:T(8,128)(2,1)}) fusion(f32[4,128,2048]{2,1,0:T(8,128)S(1)} %fusion.127, f32[4,128,2048]{2,1,0:T(8,128)} %get-tuple-element.406, bf16[4,128,640]{2,1,0:T(8,128)(2,1)S(1)} %get-tuple-element.256, bf16[2048,640,1]{1,0,2:T(8,128)(2,1)S(1)} %bitcast.585), kind=kOutput, calls=%fused_computation.49 | convolution fusion | flops 1367343104 | bytes 15859712 | tf_op jit(solution)/shard_map/bcd,fd->bcf/dot_general | solution.py:377
  276.3 4.9 fusion.3
  288.1 9.3 %collective-permute-done.32 = bf16[3,8,64,640]{3,2,1,0:T(8,128)(2,1)} collective-permute-done((bf16[3,8,64,640]{3,2,1,0:T(8,128)(2,1)}, bf16[3,8,64,640]{3,2,1,0:T(8,128)(2,1)}, u32[]{:S(2)}, u32[]{:S(2)}) %collective-permute-start.32) | collective-permute-done | bytes 1966112 | tf_op jit(solution)/shard_map/ppermute | solution.py:82
  313.4 10.2 %collective-permute-done.33 = bf16[4,128,512]{2,1,0:T(8,128)(2,1)S(1)} collective-permute-done((bf16[4,128,512]{2,1,0:T(8,128)(2,1)S(1)}, bf16[4,128,512]{2,1,0:T(8,128)(2,1)S(1)}, u32[]{:S(2)}, u32[]{:S(2)}) %collective-permute-start.33) | collective-permute-done | bytes 524320 | tf_op jit(solution)/shard_map/ppermute | solution.py:17
  338.5 4.6 multiply_convert_fusion
  360.2 4.9 collective-permute-done.37
  386.7 4.9 fusion
  398.1 9.0 %collective-permute-done.42 = bf16[3,8,64,640]{3,2,1,0:T(8,128)(2,1)} collective-permute-done((bf16[3,8,64,640]{3,2,1,0:T(8,128)(2,1)}, bf16[3,8,64,640]{3,2,1,0:T(8,128)(2,1)}, u32[]{:S(2)}, u32[]{:S(2)}) %collective-permute-start.42) | collective-permute-done | bytes 1966112 | tf_op jit(solution)/shard_map/ppermute | solution.py:82
  460.2 10.5 %collective-permute-done.54 = f32[48,128]{1,0:T(8,128)S(1)} collective-permute-done((f32[48,128]{1,0:T(8,128)S(1)}, f32[48,128]{1,0:T(8,128)S(1)}, u32[]{:S(2)}, u32[]{:S(2)}) %collective-permute-start.54) | collective-permute-done | bytes 24608 | tf_op jit(solution)/shard_map/ppermute | solution.py:82
  474.9 5.0 %collective-permute-done.55 = bf16[4,80,640]{2,1,0:T(8,128)(2,1)S(1)} collective-permute-done((bf16[4,80,640]{2,1,0:T(8,128)(2,1)S(1)}, bf16[4,80,640]{2,1,0:T(8,128)(2,1)S(1)}, u32[]{:S(2)}, u32[]{:S(2)}) %collective-permute-start.55) | collective-permute-done | bytes 409632 | tf_op jit(solution)/shard_map/ppermute | solution.py:82
  (781 shorter events, 303.8 us)
Async XLA Ops:
  4.5 25.2 %collective-permute-start = (bf16[144,640]{1,0:T(8,128)(2,1)S(1)}, bf16[144,640]{1,0:T(8,128)(2,1)S(1)}, u32[]{:S(2)}, u32[]{:S(2)}) collective-permute-start(bf16[144,640]{1,0:T(8,128)(2,1)S(1)} %get-tuple-element.283), channel_id=1, source_target_pairs={{0,2},{2,0},{4,6},{6,4},{8,10},{10,8},{12,14},{14,12},{16,18},{18,... | collective-permute-start | bytes 552968 | tf_op jit(solution)/shard_map/ppermute | solution.py:253
  5.0 24.7 %collective-permute-start.1 = (bf16[144,640]{1,0:T(8,128)(2,1)S(1)}, bf16[144,640]{1,0:T(8,128)(2,1)S(1)}, u32[]{:S(2)}, u32[]{:S(2)}) collective-permute-start(bf16[144,640]{1,0:T(8,128)(2,1)S(1)} %get-tuple-element.285), channel_id=1, source_target_pairs={{0,6},{2,4},{4,2},{6,0},{8,14},{10,12},{12,10},{14,8},{16,22},{18,... | collective-permute-start | bytes 552968 | tf_op jit(solution)/shard_map/ppermute | solution.py:253
  7.7 22.1 %collective-permute-start.2 = (bf16[144,640]{1,0:T(8,128)(2,1)S(1)}, bf16[144,640]{1,0:T(8,128)(2,1)S(1)}, u32[]{:S(2)}, u32[]{:S(2)}) collective-permute-start(bf16[144,640]{1,0:T(8,128)(2,1)S(1)} %get-tuple-element.284), channel_id=1, source_target_pairs={{0,4},{2,6},{4,0},{6,2},{8,12},{10,14},{12,8},{14,10},{16,20},{18,... | collective-permute-start | bytes 552968 | tf_op jit(solution)/shard_map/ppermute | solution.py:253
  30.4 22.8 %collective-permute-start.9 = (bf16[3,2,64,640]{3,2,0,1:T(8,128)(2,1)S(1)}, bf16[3,2,64,640]{3,2,0,1:T(8,128)(2,1)S(1)}, u32[]{:S(2)}, u32[]{:S(2)}) collective-permute-start(bf16[3,2,64,640]{3,2,0,1:T(8,128)(2,1)S(1)} %pad_maximum_fusion.23), channel_id=1, source_target_pairs={{0,8},{1,9},{2,18},{3,19},{4,12},{5,13},{6,22},{7,23},{8,0},{9,1},... | collective-permute-start | bytes 1474568 | tf_op jit(solution)/shard_map/ppermute | solution.py:82
  40.6 29.5 %collective-permute-start.7 = (bf16[16,80,640]{2,1,0:T(8,128)(2,1)S(1)}, bf16[16,80,640]{2,1,0:T(8,128)(2,1)S(1)}, u32[]{:S(2)}, u32[]{:S(2)}) collective-permute-start(bf16[16,80,640]{2,1,0:T(8,128)(2,1)S(1)} %pad_maximum_fusion.13), channel_id=1, source_target_pairs={{0,2},{1,3},{2,0},{3,1},{4,6},{5,7},{6,4},{7,5},{8,10},{9,11},{10,... | collective-permute-start | bytes 4915208 | tf_op jit(solution)/shard_map/ppermute | solution.py:82
  67.7 24.7 %collective-permute-start.11 = (bf16[3,8,64,640]{3,2,0,1:T(8,128)(2,1)S(1)}, bf16[3,8,64,640]{3,2,0,1:T(8,128)(2,1)S(1)}, u32[]{:S(2)}, u32[]{:S(2)}) collective-permute-start(bf16[3,8,64,640]{3,2,0,1:T(8,128)(2,1)S(1)} %pad_maximum_fusion.10), channel_id=1, source_target_pairs={{0,4},{1,5},{2,3},{3,2},{4,0},{5,1},{6,7},{7,6},{8,12},{9,13},{10,... | collective-permute-start | bytes 5898248 | tf_op jit(solution)/shard_map/ppermute | solution.py:82
  93.3 21.2 %collective-permute-start.13 = (bf16[3,16,64,640]{3,2,0,1:T(8,128)(2,1)S(1)}, bf16[3,16,64,640]{3,2,0,1:T(8,128)(2,1)S(1)}, u32[]{:S(2)}, u32[]{:S(2)}) collective-permute-start(bf16[3,16,64,640]{3,2,0,1:T(8,128)(2,1)S(1)} %get-tuple-element.247), channel_id=1, source_target_pairs={{0,2},{1,3},{2,0},{3,1},{4,6},{5,7},{6,4},{7,5},{8,10},{9,11},{10,... | collective-permute-start | bytes 11796488 | tf_op jit(solution)/shard_map/ppermute | solution.py:82
  94.4 14.9 %collective-permute-start.12 = (bf16[4,128,512]{2,1,0:T(8,128)(2,1)S(1)}, bf16[4,128,512]{2,1,0:T(8,128)(2,1)S(1)}, u32[]{:S(2)}, u32[]{:S(2)}) collective-permute-start(bf16[4,128,512]{2,1,0:T(8,128)(2,1)S(1)} %constant_dynamic-update-slice_fusion), channel_id=1, source_target_pairs={{0,8},{2,10},{4,12},{6,14},{8,16},{10,18},{12,20},{14,22},{16,24},... | collective-permute-start | bytes 1572872 | tf_op jit(solution)/shard_map/ppermute | solution.py:17
  116.8 26.9 %collective-permute-start.18 = (bf16[3,1,64,640]{3,2,0,1:T(8,128)(2,1)S(1)}, bf16[3,1,64,640]{3,2,0,1:T(8,128)(2,1)S(1)}, u32[]{:S(2)}, u32[]{:S(2)}) collective-permute-start(bf16[3,1,64,640]{3,2,0,1:T(8,128)(2,1)S(1)} %maximum_bitcast_fusion.1), channel_id=1, source_target_pairs={{0,16},{1,17},{2,6},{3,7},{4,20},{5,21},{6,2},{7,3},{8,24},{9,25},... | collective-permute-start | bytes 737288 | tf_op jit(solution)/shard_map/ppermute | solution.py:82
  131.9 16.4 %collective-permute-start.17 = (bf16[8,80,640]{2,1,0:T(8,128)(2,1)S(1)}, bf16[8,80,640]{2,1,0:T(8,128)(2,1)S(1)}, u32[]{:S(2)}, u32[]{:S(2)}) collective-permute-start(bf16[8,80,640]{2,1,0:T(8,128)(2,1)S(1)} %pad_maximum_fusion.18), channel_id=1, source_target_pairs={{0,4},{1,5},{2,3},{3,2},{4,0},{5,1},{6,7},{7,6},{8,12},{9,13},{10,... | collective-permute-start | bytes 2457608 | tf_op jit(solution)/shard_map/ppermute | solution.py:82
  179.8 24.7 %collective-permute-start.23 = (bf16[3,8,64,640]{3,2,0,1:T(8,128)(2,1)S(1)}, bf16[3,8,64,640]{3,2,0,1:T(8,128)(2,1)S(1)}, u32[]{:S(2)}, u32[]{:S(2)}) collective-permute-start(bf16[3,8,64,640]{3,2,0,1:T(8,128)(2,1)S(1)} %pad_maximum_fusion.11), channel_id=1, source_target_pairs={{0,4},{1,5},{2,3},{3,2},{4,0},{5,1},{6,7},{7,6},{8,12},{9,13},{10,... | collective-permute-start | bytes 5898248 | tf_op jit(solution)/shard_map/ppermute | solution.py:82
  250.4 17.1 %collective-permute-start.31 = (bf16[3,16,64,640]{3,2,1,0:T(8,128)(2,1)S(1)}, bf16[3,16,64,640]{3,2,1,0:T(8,128)(2,1)S(1)}, u32[]{:S(2)}, u32[]{:S(2)}) collective-permute-start(bf16[3,16,64,640]{3,2,1,0:T(8,128)(2,1)S(1)} %split.176), channel_id=1, source_target_pairs={{0,2},{1,3},{2,0},{3,1},{4,6},{5,7},{6,4},{7,5},{8,10},{9,11},{10,... | collective-permute-start | bytes 11796488 | tf_op jit(solution)/shard_map/ppermute | solution.py:82
  272.5 24.9 %collective-permute-start.32 = (bf16[3,8,64,640]{3,2,1,0:T(8,128)(2,1)}, bf16[3,8,64,640]{3,2,1,0:T(8,128)(2,1)}, u32[]{:S(2)}, u32[]{:S(2)}) collective-permute-start(bf16[3,8,64,640]{3,2,1,0:T(8,128)(2,1)} %split.178), channel_id=1, source_target_pairs={{0,4},{1,5},{2,3},{3,2},{4,0},{5,1},{6,7},{7,6},{8,12},{9,13},{10,... | collective-permute-start | bytes 5898248 | tf_op jit(solution)/shard_map/ppermute | solution.py:82
  306.8 16.9 %collective-permute-start.33 = (bf16[4,128,512]{2,1,0:T(8,128)(2,1)S(1)}, bf16[4,128,512]{2,1,0:T(8,128)(2,1)S(1)}, u32[]{:S(2)}, u32[]{:S(2)}) collective-permute-start(bf16[4,128,512]{2,1,0:T(8,128)(2,1)S(1)} %pad_maximum_fusion.21), channel_id=1, source_target_pairs={{8,0},{10,2},{12,4},{14,6},{16,8},{18,10},{20,12},{22,14},{24,16},... | collective-permute-start | bytes 1572872 | tf_op jit(solution)/shard_map/ppermute | solution.py:17
  311.1 23.0 %collective-permute-start.34 = (bf16[3,4,64,640]{3,2,1,0:T(8,128)(2,1)S(1)}, bf16[3,4,64,640]{3,2,1,0:T(8,128)(2,1)S(1)}, u32[]{:S(2)}, u32[]{:S(2)}) collective-permute-start(bf16[3,4,64,640]{3,2,1,0:T(8,128)(2,1)S(1)} %split.184), channel_id=1, source_target_pairs={{0,1},{1,0},{2,10},{3,11},{4,5},{5,4},{6,14},{7,15},{8,9},{9,8},{1... | collective-permute-start | bytes 2949128 | tf_op jit(solution)/shard_map/ppermute | solution.py:82
  328.6 17.3 %collective-permute-start.36 = (bf16[16,80,640]{2,1,0:T(8,128)(2,1)S(1)}, bf16[16,80,640]{2,1,0:T(8,128)(2,1)S(1)}, u32[]{:S(2)}, u32[]{:S(2)}) collective-permute-start(bf16[16,80,640]{2,1,0:T(8,128)(2,1)S(1)} %bitcast.593), channel_id=1, source_target_pairs={{0,2},{1,3},{2,0},{3,1},{4,6},{5,7},{6,4},{7,5},{8,10},{9,11},{10,... | collective-permute-start | bytes 4915208 | tf_op jit(solution)/shard_map/ppermute | solution.py:82
  351.3 27.9 %collective-permute-start.40 = (bf16[3,16,64,640]{3,2,1,0:T(8,128)(2,1)S(1)}, bf16[3,16,64,640]{3,2,1,0:T(8,128)(2,1)S(1)}, u32[]{:S(2)}, u32[]{:S(2)}) collective-permute-start(bf16[3,16,64,640]{3,2,1,0:T(8,128)(2,1)S(1)} %split.193), channel_id=1, source_target_pairs={{0,2},{1,3},{2,0},{3,1},{4,6},{5,7},{6,4},{7,5},{8,10},{9,11},{10,... | collective-permute-start | bytes 11796488 | tf_op jit(solution)/shard_map/ppermute | solution.py:82
  382.2 24.9 %collective-permute-start.42 = (bf16[3,8,64,640]{3,2,1,0:T(8,128)(2,1)}, bf16[3,8,64,640]{3,2,1,0:T(8,128)(2,1)}, u32[]{:S(2)}, u32[]{:S(2)}) collective-permute-start(bf16[3,8,64,640]{3,2,1,0:T(8,128)(2,1)} %split.197), channel_id=1, source_target_pairs={{0,4},{1,5},{2,3},{3,2},{4,0},{5,1},{6,7},{7,6},{8,12},{9,13},{10,... | collective-permute-start | bytes 5898248 | tf_op jit(solution)/shard_map/ppermute | solution.py:82
  383.7 14.5 %collective-permute-start.41 = (bf16[2,80,640]{2,1,0:T(8,128)(2,1)S(1)}, bf16[2,80,640]{2,1,0:T(8,128)(2,1)S(1)}, u32[]{:S(2)}, u32[]{:S(2)}) collective-permute-start(bf16[2,80,640]{2,1,0:T(8,128)(2,1)S(1)} %broadcast_select_fusion.19), channel_id=1, source_target_pairs={{0,8},{1,9},{2,18},{3,19},{4,12},{5,13},{6,22},{7,23},{8,0},{9,1},... | collective-permute-start | bytes 614408 | tf_op jit(solution)/shard_map/ppermute | solution.py:82
  409.3 18.4 %collective-permute-start.43 = (bf16[4,128,512]{2,1,0:T(8,128)(2,1)}, bf16[4,128,512]{2,1,0:T(8,128)(2,1)}, u32[]{:S(2)}, u32[]{:S(2)}) collective-permute-start(bf16[4,128,512]{2,1,0:T(8,128)(2,1)} %pad_maximum_fusion.22), channel_id=1, source_target_pairs={{8,0},{10,2},{12,4},{14,6},{16,8},{18,10},{20,12},{22,14},{24,16},... | collective-permute-start | bytes 1572872 | tf_op jit(solution)/shard_map/ppermute | solution.py:17
  419.7 19.9 %collective-permute-start.45 = (bf16[3,4,64,640]{3,2,1,0:T(8,128)(2,1)}, bf16[3,4,64,640]{3,2,1,0:T(8,128)(2,1)}, u32[]{:S(2)}, u32[]{:S(2)}) collective-permute-start(bf16[3,4,64,640]{3,2,1,0:T(8,128)(2,1)} %split.205), channel_id=1, source_target_pairs={{0,1},{1,0},{2,10},{3,11},{4,5},{5,4},{6,14},{7,15},{8,9},{9,8},{1... | collective-permute-start | bytes 2949128 | tf_op jit(solution)/shard_map/ppermute | solution.py:82
  421.8 17.8 %collective-permute-start.44 = (bf16[1,80,640]{2,1,0:T(8,128)(2,1)}, bf16[1,80,640]{2,1,0:T(8,128)(2,1)}, u32[]{:S(2)}, u32[]{:S(2)}) collective-permute-start(bf16[1,80,640]{2,1,0:T(8,128)(2,1)} %broadcast_select_fusion.25), channel_id=1, source_target_pairs={{0,16},{1,17},{2,6},{3,7},{4,20},{5,21},{6,2},{7,3},{8,24},{9,25},... | collective-permute-start | bytes 307208 | tf_op jit(solution)/shard_map/ppermute | solution.py:82
  437.8 17.8 %collective-permute-start.50 = (bf16[16,80,640]{2,1,0:T(8,128)(2,1)S(1)}, bf16[16,80,640]{2,1,0:T(8,128)(2,1)S(1)}, u32[]{:S(2)}, u32[]{:S(2)}) collective-permute-start(bf16[16,80,640]{2,1,0:T(8,128)(2,1)S(1)} %bitcast.592), channel_id=1, source_target_pairs={{0,2},{1,3},{2,0},{3,1},{4,6},{5,7},{6,4},{7,5},{8,10},{9,11},{10,... | collective-permute-start | bytes 4915208 | tf_op jit(solution)/shard_map/ppermute | solution.py:82
  456.0 14.7 %collective-permute-start.53 = (bf16[8,80,640]{2,1,0:T(8,128)(2,1)S(1)}, bf16[8,80,640]{2,1,0:T(8,128)(2,1)S(1)}, u32[]{:S(2)}, u32[]{:S(2)}) collective-permute-start(bf16[8,80,640]{2,1,0:T(8,128)(2,1)S(1)} %broadcast_select_fusion.6), channel_id=1, source_target_pairs={{0,4},{1,5},{2,3},{3,2},{4,0},{5,1},{6,7},{7,6},{8,12},{9,13},{10,... | collective-permute-start | bytes 2457608 | tf_op jit(solution)/shard_map/ppermute | solution.py:82
  (209 other events, 2223.3 us)
